TPU v7x, 32 devices: a whole 2x2x4 slice. The times are simulated.
32 devices in a mesh: row: 8 (over z, x), col: 4 (over y, core).
Axes of the slice: x: 2, y: 2, z: 4, core: 2. Of those that a mesh axis runs over, the one named last changes fastest.
Arguments:
- density: bfloat16 [4096, 1536], P(('row', 'col')), may hold values from -0.625 to 0.625
- pattern: int32 [32, 12], P(('row', 'col')), may hold values from 0 to 1, as said below
Outputs:
- band: bfloat16 [4096, 8, 512], P('row', None, 'col')
Inputs may be any that keep to these rules, and one draw needn't show every extreme that they name: `pattern`: each block row has its own share of stored blocks.
All inputs are finite; a program needn't handle non-finite values.
Results may differ from a plain program's by a relative error of at most 0.001.
Values may be sent and summed in bfloat16 or wider, within the bound.
A program may use at most 64 MiB of HBM per device.

v0:
```python
import jax
import jax.numpy as jnp
from jax import lax
from jax.sharding import PartitionSpec as P


def from_behind(value, axis, steps):
    count = lax.axis_size(axis)
    pairs = [(source, (source + steps) % count) for source in range(count)]
    return lax.ppermute(value, axis, pairs)


def local(density, pattern):
    block_rows = density.shape[0]
    width_all = density.shape[1]
    offsets_total = lax.axis_size("row")
    half_span = lax.axis_size("row") // 4
    present = pattern.reshape(1, width_all // block_rows, 1).astype(jnp.bfloat16)
    masked = (density.reshape(block_rows, width_all // block_rows, block_rows) * present).reshape(
        block_rows, width_all
    )
    upward = []
    current = masked
    for turn_index in range(half_span):
        current = from_behind(current, "row", -1)
        upward.append(current)
    panels = upward[::-1] + [masked]
    current = masked
    for turn_index in range(offsets_total - half_span - 1):
        current = from_behind(current, "row", 1)
        panels.append(current)
    gathered = lax.all_gather(masked, "col", axis=0, tiled=True)
    results = []
    for partner in panels:
        product = lax.dot_general(
            gathered, partner, (((1,), (1,)), ((), ())), preferred_element_type=jnp.float32
        )
        results.append(product.astype(jnp.bfloat16))
    return jnp.stack(results, axis=1)


def solution(mesh):
    return jax.shard_map(
        local,
        mesh=mesh,
        in_specs=(P(("row", "col"), None), P(("row", "col"), None)),
        out_specs=P("row", None, "col"),
        check_vma=False,
    )
```

profile of v0, /device:TPU:0, one launch (start us, length us, event | category | flops | bytes accessed | tf_op | source)
XLA Modules:
  0.0 93.8 jit_solution(18000753571964377312)
XLA Ops:
  6.5 0.7 convert_bitcast_fusion
  7.2 0.1 broadcast_bitcast_fusion
  7.3 1.8 %broadcast_multiply_fusion = bf16[128,1536]{1,0:T(8,128)(2,1)} fusion(bf16[128,1536]{1,0:T(8,128)(2,1)} %param.2, bf16[1536]{0:T(1024)(128)(2,1)S(1)} %broadcast_bitcast_fusion), kind=kLoop, calls=%fused_computation.24 | loop fusion | flops 196608 | bytes 789504 | tf_op jit(solution)/shard_map/mul | solution.py:19
  9.1 3.0 %collective-permute-start.2 = (bf16[128,1536]{1,0:T(8,128)(2,1)}, bf16[128,1536]{1,0:T(8,128)(2,1)S(1)}, u32[]{:S(2)}, u32[]{:S(2)}) collective-permute-start(bf16[128,1536]{1,0:T(8,128)(2,1)} %broadcast_multiply_fusion), channel_id=1, source_target_pairs={{0,4},{4,8},{8,12},{12,16},{16,20},{20,24},{24,28},{28,0},{1,5},{5... | collective-permute-start | bytes 1179656 | tf_op jit(solution)/shard_map/ppermute | solution.py:10
  12.1 12.4 %collective-permute-done.2 = bf16[128,1536]{1,0:T(8,128)(2,1)S(1)} collective-permute-done((bf16[128,1536]{1,0:T(8,128)(2,1)}, bf16[128,1536]{1,0:T(8,128)(2,1)S(1)}, u32[]{:S(2)}, u32[]{:S(2)}) %collective-permute-start.2) | collective-permute-done | bytes 393248 | tf_op jit(solution)/shard_map/ppermute | solution.py:10
  24.4 13.0 %collective-permute-done.3 = bf16[128,1536]{1,0:T(8,128)(2,1)S(1)} collective-permute-done((bf16[128,1536]{1,0:T(8,128)(2,1)S(1)}, bf16[128,1536]{1,0:T(8,128)(2,1)S(1)}, u32[]{:S(2)}, u32[]{:S(2)}) %collective-permute-start.3) | collective-permute-done | bytes 393248 | tf_op jit(solution)/shard_map/ppermute | solution.py:10
  37.4 4.7 %collective-permute-start = (bf16[128,1536]{1,0:T(8,128)(2,1)}, bf16[128,1536]{1,0:T(8,128)(2,1)S(1)}, u32[]{:S(2)}, u32[]{:S(2)}) collective-permute-start(bf16[128,1536]{1,0:T(8,128)(2,1)} %broadcast_multiply_fusion), channel_id=1, source_target_pairs={{0,28},{4,0},{8,4},{12,8},{16,12},{20,16},{24,20},{28,24},{1,29},{... | collective-permute-start | bytes 1179656 | tf_op jit(solution)/shard_map/ppermute | solution.py:10
  42.1 10.1 %collective-permute-done.4 = bf16[128,1536]{1,0:T(8,128)(2,1)S(1)} collective-permute-done((bf16[128,1536]{1,0:T(8,128)(2,1)S(1)}, bf16[128,1536]{1,0:T(8,128)(2,1)S(1)}, u32[]{:S(2)}, u32[]{:S(2)}) %collective-permute-start.4) | collective-permute-done | bytes 393248 | tf_op jit(solution)/shard_map/ppermute | solution.py:10
  52.3 2.5 %collective-permute-start.5 = (bf16[128,1536]{1,0:T(8,128)(2,1)S(1)}, bf16[128,1536]{1,0:T(8,128)(2,1)S(1)}, u32[]{:S(2)}, u32[]{:S(2)}) collective-permute-start(bf16[128,1536]{1,0:T(8,128)(2,1)S(1)} %collective-permute-done.4), channel_id=1, source_target_pairs={{0,4},{4,8},{8,12},{12,16},{16,20},{20,24},{24,28},{28,0},{1,5},{5... | collective-permute-start | bytes 1179656 | tf_op jit(solution)/shard_map/ppermute | solution.py:10
  54.8 0.7 collective-permute-done
  55.4 7.5 %collective-permute-start.1 = (bf16[128,1536]{1,0:T(8,128)(2,1)S(1)}, bf16[128,1536]{1,0:T(8,128)(2,1)S(1)}, u32[]{:S(2)}, u32[]{:S(2)}) collective-permute-start(bf16[128,1536]{1,0:T(8,128)(2,1)S(1)} %collective-permute-done), channel_id=1, source_target_pairs={{0,28},{4,0},{8,4},{12,8},{16,12},{20,16},{24,20},{28,24},{1,29},{... | collective-permute-start | bytes 1179656 | tf_op jit(solution)/shard_map/ppermute | solution.py:10
  62.9 8.8 %collective-permute-done.5 = bf16[128,1536]{1,0:T(8,128)(2,1)S(1)} collective-permute-done((bf16[128,1536]{1,0:T(8,128)(2,1)S(1)}, bf16[128,1536]{1,0:T(8,128)(2,1)S(1)}, u32[]{:S(2)}, u32[]{:S(2)}) %collective-permute-start.5) | collective-permute-done | bytes 393248 | tf_op jit(solution)/shard_map/ppermute | solution.py:10
  71.8 2.5 %collective-permute-start.6 = (bf16[128,1536]{1,0:T(8,128)(2,1)S(1)}, bf16[128,1536]{1,0:T(8,128)(2,1)S(1)}, u32[]{:S(2)}, u32[]{:S(2)}) collective-permute-start(bf16[128,1536]{1,0:T(8,128)(2,1)S(1)} %collective-permute-done.5), channel_id=1, source_target_pairs={{0,4},{4,8},{8,12},{12,16},{16,20},{20,24},{24,28},{28,0},{1,5},{5... | collective-permute-start | bytes 1179656 | tf_op jit(solution)/shard_map/ppermute | solution.py:10
  74.2 2.1 %fusion.1 = bf16[512,8,128]{2,0,1:T(8,128)(2,1)S(1)} fusion(bf16[512,1536]{1,0:T(8,128)(2,1)} %all-gather.2.cloned.1.call-done, bf16[128,1536]{1,0:T(8,128)(2,1)S(1)} %collective-permute-done.1), kind=kOutput, calls=%fused_computation.9 | convolution fusion | flops 201392128 | bytes 2097152 | tf_op jit(solution)/shard_map/dot_general | solution.py:35
  76.4 0.6 fusion.3
  77.0 0.4 copy-done.1
  77.4 0.6 fusion.5
  78.0 0.6 fusion.7
  78.6 0.6 fusion.9
  79.2 0.6 fusion.11
  79.8 0.6 fusion.13
  80.5 4.2 %collective-permute-done.6 = bf16[128,1536]{1,0:T(8,128)(2,1)S(1)} collective-permute-done((bf16[128,1536]{1,0:T(8,128)(2,1)S(1)}, bf16[128,1536]{1,0:T(8,128)(2,1)S(1)}, u32[]{:S(2)}, u32[]{:S(2)}) %collective-permute-start.6) | collective-permute-done | bytes 393248 | tf_op jit(solution)/shard_map/ppermute | solution.py:10
  84.7 0.6 fusion.15
  85.3 1.7 %copy.3 = bf16[512,8,128]{2,1,0:T(8,128)(2,1)} copy(bf16[512,8,128]{2,0,1:T(8,128)(2,1)S(1)} %fusion.15) | data formatting | bytes 2097152 | tf_op jit(solution)/shard_map/stack | solution.py:39
  (9 shorter events, 0.0 us)
Async XLA Ops:
  6.5 67.7 %all-gather.2.cloned.1.call-start = ((), (), s32[]{:S(2)}) async-start(), calls=%async_computation | async-start | bytes 1966080 | tf_op jit(solution)/shard_map/all_gather | solution.py:32
  9.1 15.4 %collective-permute-start.2 = (bf16[128,1536]{1,0:T(8,128)(2,1)}, bf16[128,1536]{1,0:T(8,128)(2,1)S(1)}, u32[]{:S(2)}, u32[]{:S(2)}) collective-permute-start(bf16[128,1536]{1,0:T(8,128)(2,1)} %broadcast_multiply_fusion), channel_id=1, source_target_pairs={{0,4},{4,8},{8,12},{12,16},{16,20},{20,24},{24,28},{28,0},{1,5},{5... | collective-permute-start | bytes 1179656 | tf_op jit(solution)/shard_map/ppermute | solution.py:10
  24.4 13.0 %collective-permute-start.3 = (bf16[128,1536]{1,0:T(8,128)(2,1)S(1)}, bf16[128,1536]{1,0:T(8,128)(2,1)S(1)}, u32[]{:S(2)}, u32[]{:S(2)}) collective-permute-start(bf16[128,1536]{1,0:T(8,128)(2,1)S(1)} %collective-permute-done.2), channel_id=1, source_target_pairs={{0,4},{4,8},{8,12},{12,16},{16,20},{20,24},{24,28},{28,0},{1,5},{5... | collective-permute-start | bytes 1179656 | tf_op jit(solution)/shard_map/ppermute | solution.py:10
  37.4 14.9 %collective-permute-start.4 = (bf16[128,1536]{1,0:T(8,128)(2,1)S(1)}, bf16[128,1536]{1,0:T(8,128)(2,1)S(1)}, u32[]{:S(2)}, u32[]{:S(2)}) collective-permute-start(bf16[128,1536]{1,0:T(8,128)(2,1)S(1)} %collective-permute-done.3), channel_id=1, source_target_pairs={{0,4},{4,8},{8,12},{12,16},{16,20},{20,24},{24,28},{28,0},{1,5},{5... | collective-permute-start | bytes 1179656 | tf_op jit(solution)/shard_map/ppermute | solution.py:10
  37.4 18.0 %collective-permute-start = (bf16[128,1536]{1,0:T(8,128)(2,1)}, bf16[128,1536]{1,0:T(8,128)(2,1)S(1)}, u32[]{:S(2)}, u32[]{:S(2)}) collective-permute-start(bf16[128,1536]{1,0:T(8,128)(2,1)} %broadcast_multiply_fusion), channel_id=1, source_target_pairs={{0,28},{4,0},{8,4},{12,8},{16,12},{20,16},{24,20},{28,24},{1,29},{... | collective-permute-start | bytes 1179656 | tf_op jit(solution)/shard_map/ppermute | solution.py:10
  52.3 19.5 %collective-permute-start.5 = (bf16[128,1536]{1,0:T(8,128)(2,1)S(1)}, bf16[128,1536]{1,0:T(8,128)(2,1)S(1)}, u32[]{:S(2)}, u32[]{:S(2)}) collective-permute-start(bf16[128,1536]{1,0:T(8,128)(2,1)S(1)} %collective-permute-done.4), channel_id=1, source_target_pairs={{0,4},{4,8},{8,12},{12,16},{16,20},{20,24},{24,28},{28,0},{1,5},{5... | collective-permute-start | bytes 1179656 | tf_op jit(solution)/shard_map/ppermute | solution.py:10
  55.4 18.8 %collective-permute-start.1 = (bf16[128,1536]{1,0:T(8,128)(2,1)S(1)}, bf16[128,1536]{1,0:T(8,128)(2,1)S(1)}, u32[]{:S(2)}, u32[]{:S(2)}) collective-permute-start(bf16[128,1536]{1,0:T(8,128)(2,1)S(1)} %collective-permute-done), channel_id=1, source_target_pairs={{0,28},{4,0},{8,4},{12,8},{16,12},{20,16},{24,20},{28,24},{1,29},{... | collective-permute-start | bytes 1179656 | tf_op jit(solution)/shard_map/ppermute | solution.py:10
  71.8 12.9 %collective-permute-start.6 = (bf16[128,1536]{1,0:T(8,128)(2,1)S(1)}, bf16[128,1536]{1,0:T(8,128)(2,1)S(1)}, u32[]{:S(2)}, u32[]{:S(2)}) collective-permute-start(bf16[128,1536]{1,0:T(8,128)(2,1)S(1)} %collective-permute-done.5), channel_id=1, source_target_pairs={{0,4},{4,8},{8,12},{12,16},{16,20},{20,24},{24,28},{28,0},{1,5},{5... | collective-permute-start | bytes 1179656 | tf_op jit(solution)/shard_map/ppermute | solution.py:10
  74.2 2.1 %copy-start = (bf16[512,1536]{1,0:T(8,128)(2,1)S(1)}, bf16[512,1536]{1,0:T(8,128)(2,1)}, u32[]{:S(2)}) copy-start(bf16[512,1536]{1,0:T(8,128)(2,1)} %all-gather.2.cloned.1.call-done) | copy-start | bytes 4718596
  76.4 1.0 %copy-start.1 = (bf16[128,1536]{1,0:T(8,128)(2,1)S(1)}, bf16[128,1536]{1,0:T(8,128)(2,1)}, u32[]{:S(2)}) copy-start(bf16[128,1536]{1,0:T(8,128)(2,1)} %broadcast_multiply_fusion) | copy-start | bytes 1179652
Sparse Core Ops, SparseCore 0:
  9.2 22.3 all-gather.1
where the time goes:
time: 94 us; the launch traced here: 93.8 us
  waiting for transfers between devices  49.2 us (52%)
  starting transfers between devices  20.2 us (21%)
  between operations  13.5 us (14%)
  matrix products  6.41 us (7%)
  other arithmetic  2.43 us (3%)
  local copies, waits for them, and re-layouts  2.1 us (2%)
    ppermute x7, waiting for transfers between devices, from_behind(): return lax.ppermute(value, axis, pairs)  49.2 us
    ppermute x7, starting transfers between devices, from_behind(): return lax.ppermute(value, axis, pairs)  20.2 us
    dot_general x8, matrix products, local(): lax.dot_general(gathered, partner, (((1,), (1,)), ((), ())), preferred_el...  6.41 us
  transfers between devices with their start and end apart: 8, of which 6 were waited for; matrix products, arithmetic and copies ran while one was open for 6% of the time, Pallas kernels for 0%

commit v1 on v0

v1 whole, which is shorter than its diff:
```python
import functools

import jax
import jax.numpy as jnp
from jax import lax
from jax.experimental import pallas as pl
from jax.experimental.pallas import tpu as pltpu
from jax.sharding import PartitionSpec as P

MESH = pl.DeviceIdType.MESH
CHUNKS = 2


def kernel(
    rows_n, cols_n, dens, pat, out, rowb, gb, ob, pb,
    r_row, r_gb, r_ob, s_up, s_dn, s_dup, s_x, s_y, s_c, s_p, s_out,
):
    zn, yn = rows_n // 2, cols_n // 2
    length, width = dens.shape
    group = cols_n * length
    part = length // CHUNKS
    half_span = rows_n // 4
    g, c = lax.axis_index("row"), lax.axis_index("col")
    z, x = g // 2, lax.rem(g, 2)
    y, k = c // 2, lax.rem(c, 2)
    low, high = z == 0, z == zn - 1
    edge = low | high
    inner = jnp.logical_not(edge)
    proxy = (z == 1) | (z == zn - 2)
    away = jnp.where((z == 1) | low, 1, jnp.where((z == zn - 2) | high, -1, 1))
    inward = z + away
    ze = z - away

    def row_of(zz, xx):
        return zz * 2 + xx

    def when(cond, action):
        pl.when(cond)(action)

    def dev_z(zz):
        return (row_of(zz, x), c)

    dev_x = (row_of(z, 1 - x), c)
    dev_k = (g, y * 2 + 1 - k)

    def dev_y(d):
        return (g, lax.rem(y + d, yn) * 2 + k)

    barrier = pltpu.get_barrier_semaphore()

    def greet(device):
        pl.semaphore_signal(barrier, inc=1, device_id=device, device_id_type=MESH)

    greet(dev_x)
    greet(dev_k)
    for d in range(1, yn):
        greet(dev_y(d))
    when(z > 0, lambda: greet(dev_z(z - 1)))
    when(z < zn - 1, lambda: greet(dev_z(z + 1)))

    def rows_at(n):
        return pl.ds(n * part, part)

    def gb_rows(cc, n):
        return pl.ds(pl.multiple_of(cc * length + n * part, part), part)

    blocks = pat.shape[0]
    size = length // blocks
    c0 = pl.multiple_of(c * length, length)
    for b in range(blocks):
        for kb in range(pat.shape[1]):
            here = dens[b * size:(b + 1) * size, kb * size:(kb + 1) * size]
            keep = jnp.broadcast_to(pat[b:b + 1, kb:kb + 1], here.shape) != 0
            kept = jnp.where(keep, here.astype(jnp.float32), 0.0).astype(here.dtype)
            rowb[z, x, b * size:(b + 1) * size, kb * size:(kb + 1) * size] = kept
            gb[0, pl.ds(c0 + b * size, size), kb * size:(kb + 1) * size] = kept

    def remote(src, dst, send, recv, device):
        return pltpu.make_async_remote_copy(
            src_ref=src, dst_ref=dst, send_sem=send, recv_sem=recv,
            device_id=device, device_id_type=MESH,
        )

    def row_copy(zz, xx, n, send, device):
        ref = rowb.at[zz, xx, rows_at(n)]
        return remote(ref, ref, send, r_row.at[zz, xx, n], device)

    def up(zz, n):
        return row_copy(zz, x, n, s_up.at[zz, n], dev_z(z + 1))

    def down(zz, n):
        return row_copy(zz, x, n, s_dn.at[zz, n], dev_z(z - 1))

    def double(n):
        return row_copy(z, 1 - x, n, s_dup.at[n], dev_z(inward))

    def across(zz, n):
        return row_copy(zz, x, n, s_x.at[zz, n], dev_x)

    def gb_send(p, src, cc, n, send, device):
        return remote(src, gb.at[p, gb_rows(cc, n)], send, r_gb.at[p, cc, n], device)

    def sideways(p, d, n):
        src = gb.at[0, gb_rows(c, n)] if p == 0 else rowb.at[ze, x, rows_at(n)]
        return gb_send(p, src, c, n, s_y.at[p, d, n], dev_y(d))

    def to_twin(p, d, n):
        cc = lax.rem(y + d, yn) * 2 + k
        if p == 1 and d == 0:
            src = rowb.at[ze, x, rows_at(n)]
        else:
            src = gb.at[p, gb_rows(cc, n)]
        return gb_send(p, src, cc, n, s_c.at[p, d, n], dev_k)

    def got_row(zz, xx, n):
        row_copy(zz, xx, n, s_dup.at[n], dev_x).wait_recv()

    def got_gb(p, cc, n):
        ref = gb.at[p, gb_rows(cc, n)]
        remote(ref, ref, s_dup.at[n], r_gb.at[p, cc, n], dev_x).wait_recv()

    def own_sends(n, do):
        for d in range(1, yn):
            do(sideways(0, d, n))
        do(across(z, n))
        when(z < zn - 1, lambda: do(up(z, n)))
        when(z > 0, lambda: do(down(z, n)))
        do(to_twin(0, 0, n))

    def y_arrivals(p, n, do, wait):
        for d in range(1, yn):
            if wait:
                got_gb(p, lax.rem(y + d, yn) * 2 + k, n)
            do(to_twin(p, d, n))

    def relay(zz, n, do):
        @pl.when((zz < z) & (z + 1 <= zn - 2))
        def _():
            do(up(zz, n))

        @pl.when((zz > z) & (z - 1 >= 1))
        def _():
            do(down(zz, n))

        adjacent = proxy & (zz == ze)

        @pl.when(jnp.logical_not(adjacent))
        def _():
            do(across(zz, n))

        @pl.when(adjacent)
        def _():
            for d in range(1, yn):
                do(sideways(1, d, n))
            do(to_twin(1, 0, n))

    def inside(zz):
        return (zz >= 0) & (zz <= zn - 1)

    def start(copy):
        copy.start()

    def finish(copy):
        copy.wait_send()

    step_rows = min(group, 512)

    def product(p, zz, xx, target, slot):
        def body(i, carry):
            at = pl.ds(pl.multiple_of(i * step_rows, step_rows), step_rows)
            target[slot, at, :] = lax.dot_general(
                gb[p, at, :], rowb[zz, xx], (((1,), (1,)), ((), ())),
                preferred_element_type=jnp.float32,
            ).astype(target.dtype)
            return carry

        if group == step_rows:
            body(0, 0)
        else:
            lax.fori_loop(0, group // step_rows, body, 0)

    def slot_of(gg, q):
        return lax.rem(gg + half_span - q + rows_n, rows_n)

    def out_copy(s):
        return pltpu.make_async_copy(ob.at[s], out.at[s], s_out.at[s])

    def own_job(zz, xx):
        s = slot_of(g, row_of(zz, xx))
        product(0, zz, xx, ob, s)
        out_copy(s).start()

    def proxy_copy(q):
        s = slot_of(row_of(ze, x), q)
        return remote(pb.at[q], ob.at[s], s_p.at[q], r_ob.at[s], dev_z(ze))

    def proxy_job(zz, xx):
        q = row_of(zz, xx)
        product(1, zz, xx, pb, q)
        proxy_copy(q).start()

    def all_twin(p):
        for n in range(CHUNKS):
            for d in range(yn):
                got_gb(p, lax.rem(y + d, yn) * 2 + 1 - k, n)

    neighbours = 2 + (yn - 1)
    pl.semaphore_wait(barrier, neighbours + jnp.where(edge, 1, 2))

    for n in range(CHUNKS):
        own_sends(n, start)

    @pl.when(edge)
    def _():
        for n in range(CHUNKS):
            y_arrivals(0, n, start, True)
            got_row(z, 1 - x, n)
            double(n).start()
            got_row(inward, x, n)
            across(inward, n).start()
        all_twin(0)

        def job(j, carry):
            zz = jnp.where(j < 2, z, inward)
            xx = jnp.where(lax.rem(j, 2) == 0, x, 1 - x)

            @pl.when(j == 3)
            def _():
                for n in range(CHUNKS):
                    got_row(inward, 1 - x, n)

            own_job(zz, xx)
            return carry

        lax.fori_loop(0, 4, job, 0)

        def far(i, carry):
            zz = inward + away * (i // 2 + 1)
            xx = jnp.where(lax.rem(i, 2) == 0, x, 1 - x)
            s = slot_of(g, row_of(zz, xx))
            remote(ob.at[s], ob.at[s], s_p.at[0], r_ob.at[s], dev_x).wait_recv()
            out_copy(s).start()
            return carry

        lax.fori_loop(0, 2 * (zn - 2), far, 0)

    @pl.when(inner)
    def _():
        def turn(t, carry):
            for n in range(CHUNKS):
                @pl.when(t == 1)
                def _():
                    y_arrivals(0, n, start, True)

                @pl.when((t == 2) & proxy)
                def _():
                    y_arrivals(1, n, start, True)

                for zz in (z - t * away, z + t * away):
                    @pl.when(inside(zz))
                    def _():
                        got_row(zz, x, n)
                        relay(zz, n, start)

            @pl.when(t == 1)
            def _():
                all_twin(0)

            @pl.when((t == 2) & proxy)
            def _():
                gb[1, pl.ds(c0, length), :] = rowb[ze, x]
                all_twin(1)

            def job(j, inner_carry):
                dist = jnp.where(j < 3, t - 1, t)
                sign = jnp.where((j == 2) | (j == 4), -away, away)
                zz = z + sign * dist
                other = (j == 1) | (j == 2)
                xx = jnp.where(other, 1 - x, x)
                valid = inside(zz) & jnp.where(
                    j == 0, t <= 2, jnp.where(j == 2, t >= 2, True)
                )

                @pl.when(valid & other)
                def _():
                    for n in range(CHUNKS):
                        got_row(zz, 1 - x, n)

                @pl.when(
                    valid & proxy & (t >= 2) & ((j == 0) | (j == 1) | (j == 3))
                )
                def _():
                    proxy_job(zz, xx)

                @pl.when(valid & jnp.where(j == 0, t == 1, True))
                def _():
                    own_job(zz, xx)

                return inner_carry

            lax.fori_loop(0, 5, job, 0)
            return carry

        lax.fori_loop(1, zn, turn, 0)

    for n in range(CHUNKS):
        own_sends(n, finish)
        y_arrivals(0, n, finish, False)

    @pl.when(edge)
    def _():
        for n in range(CHUNKS):
            double(n).wait_send()
            across(inward, n).wait_send()

    @pl.when(inner)
    def _():
        @pl.when(proxy)
        def _():
            for n in range(CHUNKS):
                y_arrivals(1, n, finish, False)

            def sent(i, carry):
                zz = z + away * (i // 2 + 1)
                proxy_copy(row_of(zz, lax.rem(i, 2))).wait_send()
                return carry

            lax.fori_loop(0, 2 * (zn - 2), sent, 0)

        def relayed(zz, carry):
            @pl.when(zz != z)
            def _():
                for n in range(CHUNKS):
                    relay(zz, n, finish)

            return carry

        lax.fori_loop(0, zn, relayed, 0)

    def stored(s, carry):
        out_copy(s).wait()
        return carry

    lax.fori_loop(0, rows_n, stored, 0)


def local(density, pattern):
    rows_n, cols_n = lax.axis_size("row"), lax.axis_size("col")
    length, width = density.shape
    group = cols_n * length
    zn, yn = rows_n // 2, cols_n // 2
    kind = density.dtype
    dma = pltpu.SemaphoreType.DMA
    words = (2 * rows_n * group * length + (2 * group + rows_n * length + 2 * length) * width)
    out = pl.pallas_call(
        functools.partial(kernel, rows_n, cols_n),
        out_shape=jax.ShapeDtypeStruct((rows_n, group, length), kind),
        in_specs=[pl.BlockSpec(memory_space=pltpu.VMEM)] * 2,
        out_specs=pl.BlockSpec(memory_space=pl.ANY),
        scratch_shapes=[
            pltpu.VMEM((zn, 2, length, width), kind),
            pltpu.VMEM((2, group, width), kind),
            pltpu.VMEM((rows_n, group, length), kind),
            pltpu.VMEM((rows_n, group, length), kind),
            dma((zn, 2, CHUNKS)),
            dma((2, cols_n, CHUNKS)),
            dma((rows_n,)),
            dma((zn, CHUNKS)),
            dma((zn, CHUNKS)),
            dma((CHUNKS,)),
            dma((zn, CHUNKS)),
            dma((2, yn, CHUNKS)),
            dma((2, yn, CHUNKS)),
            dma((rows_n,)),
            dma((rows_n,)),
        ],
        compiler_params=pltpu.CompilerParams(
            collective_id=0, has_side_effects=True, vmem_limit_bytes=2 * words + (8 << 20)
        ),
        cost_estimate=pl.CostEstimate(
            flops=2 * group * length * width * rows_n,
            bytes_accessed=2 * rows_n * group * length,
            transcendentals=0,
        ),
    )(density, pattern)
    return jnp.transpose(out, (1, 0, 2))


def solution(mesh):
    return jax.shard_map(
        local,
        mesh=mesh,
        in_specs=(P(("row", "col"), None), P(("row", "col"), None)),
        out_specs=P("row", None, "col"),
        check_vma=False,
    )
```

time: 94 us -> 41.3 us (0.44)
  waiting for transfers between devices: 49.2 us -> 0 us
  Pallas kernels: 0 us -> 37.8 us
  starting transfers between devices: 20.2 us -> 0 us
  between operations: 13.5 us -> 0.01 us
  matrix products: 6.41 us -> 0 us
  other arithmetic: 2.43 us -> 0 us
  local copies, waits for them, and re-layouts: 2.1 us -> 3.3 us
    ppermute x7 -> x0, waiting for transfers between devices: 49.2 us -> none  [from_behind(): return lax.ppermute(value, axis, pairs)]
    pallas_call x0 -> x1, Pallas kernels: none -> 37.8 us  [local(): pl.pallas_call(functools.partial(kernel, rows_n, cols_n), out_shape=jax.S...]
    ppermute x7 -> x0, starting transfers between devices: 20.2 us -> none  [from_behind(): return lax.ppermute(value, axis, pairs)]
    dot_general x8 -> x0, matrix products: 6.41 us -> none  [local(): lax.dot_general(gathered, partner, (((1,), (1,)), ((), ())), preferred_el...]
    mul x1 -> x0, other arithmetic: 1.77 us -> none  [local(): density.reshape(block_rows, width_all // block_rows, block_rows) * present]
    another operation x1 -> x0, local copies, waits for them, and re-layouts: 1.65 us -> none  [local(): return jnp.stack(results, axis=1)]
    transpose x0 -> x1, local copies, waits for them, and re-layouts: none -> 1.65 us  [local(): return jnp.transpose(out, (1, 0, 2))]
    unnamed x4, local copies, waits for them, and re-layouts: 0.37 us -> 1.65 us
  transfers between devices with their start and end apart: 8 -> 0, of which waited for: 6 -> 0; matrix products, arithmetic and copies ran while one was open for 6% -> 0% of each run, Pallas kernels for 0% -> 0%
where the time goes in v1:
time: 41.3 us; the launch traced here: 41.2 us
  Pallas kernels  37.8 us (92%)
  local copies, waits for them, and re-layouts  3.3 us (8%)
    pallas_call x1, Pallas kernels, local(): pl.pallas_call(functools.partial(kernel, rows_n, cols_n), out_shape=jax.S...  37.8 us
    unnamed x4, local copies, waits for them, and re-layouts  1.65 us
    transpose x1, local copies, waits for them, and re-layouts, local(): return jnp.transpose(out, (1, 0, 2))  1.65 us

profile of v1, /device:TPU:0, one launch (start us, length us, event | category | flops | bytes accessed | tf_op | source)
XLA Modules:
  0.0 41.2 jit_solution(7375069345927234935)
XLA Ops:
  0.0 0.0 copy-start
  0.0 1.0 %copy-done = bf16[128,1536]{1,0:T(8,128)(2,1)S(1)} copy-done((bf16[128,1536]{1,0:T(8,128)(2,1)S(1)}, bf16[128,1536]{1,0:T(8,128)(2,1)}, u32[]{:S(2)}) %copy-start) | copy-done | bytes 393240
  1.0 0.0 copy-start.1
  1.0 0.7 %copy-done.1 = s32[1,12]{1,0:T(1,128)S(1)} copy-done((s32[1,12]{1,0:T(1,128)S(1)}, s32[1,12]{1,0:T(1,128)}, u32[]{:S(2)}) %copy-start.1) | copy-done | bytes 72
  1.7 37.8 %shard_map.28 = bf16[8,512,128]{2,1,0:T(8,128)(2,1)S(1)} custom-call(bf16[128,1536]{1,0:T(8,128)(2,1)S(1)} %copy-done, s32[1,12]{1,0:T(1,128)S(1)} %copy-done.1), custom_call_target="tpu_custom_call" | custom-call | flops 1610612736 | bytes 1048576 | tf_op jit(solution)/shard_map/pallas_call | solution.py:355
  39.5 1.6 %copy.3 = bf16[512,8,128]{2,1,0:T(8,128)(2,1)} copy(bf16[512,8,128]{2,0,1:T(8,128)(2,1)S(1)} %bitcast.1) | data formatting | bytes 2097152 | tf_op jit(solution)/shard_map/transpose | solution.py:386
Async XLA Ops:
  0.0 1.0 %copy-start = (bf16[128,1536]{1,0:T(8,128)(2,1)S(1)}, bf16[128,1536]{1,0:T(8,128)(2,1)}, u32[]{:S(2)}) copy-start(bf16[128,1536]{1,0:T(8,128)(2,1)} %dens.1) | copy-start | bytes 1179652
  1.0 0.7 %copy-start.1 = (s32[1,12]{1,0:T(1,128)S(1)}, s32[1,12]{1,0:T(1,128)}, u32[]{:S(2)}) copy-start(s32[1,12]{1,0:T(1,128)} %pat.1) | copy-start | bytes 148

commit v2 on v1

--- a/solution.py
+++ b/solution.py
@@ -8,13 +8,18 @@
 from jax.sharding import PartitionSpec as P
 
 MESH = pl.DeviceIdType.MESH
-CHUNKS = 2
+CHUNKS = 4
+HALF = CHUNKS // 2
 
 
 def kernel(
-    rows_n, cols_n, dens, pat, out, rowb, gb, ob, pb,
+    rows_n, cols_n, dens_hbm, pat_hbm, out, dens, pat, rowb, gb, ob, pb, s_in,
     r_row, r_gb, r_ob, s_up, s_dn, s_dup, s_x, s_y, s_c, s_p, s_out,
 ):
+    fetch_dens = pltpu.make_async_copy(dens_hbm, dens, s_in.at[0])
+    fetch_pat = pltpu.make_async_copy(pat_hbm, pat, s_in.at[1])
+    fetch_dens.start()
+    fetch_pat.start()
     zn, yn = rows_n // 2, cols_n // 2
     length, width = dens.shape
     group = cols_n * length
@@ -58,8 +63,8 @@
     when(z > 0, lambda: greet(dev_z(z - 1)))
     when(z < zn - 1, lambda: greet(dev_z(z + 1)))
 
-    def rows_at(n):
-        return pl.ds(n * part, part)
+    def rows_at(xx, n):
+        return pl.ds(pl.multiple_of(xx * length + n * part, part), part)
 
     def gb_rows(cc, n):
         return pl.ds(pl.multiple_of(cc * length + n * part, part), part)
@@ -67,12 +72,15 @@
     blocks = pat.shape[0]
     size = length // blocks
     c0 = pl.multiple_of(c * length, length)
+    x0 = pl.multiple_of(x * length, length)
+    fetch_dens.wait()
+    fetch_pat.wait()
     for b in range(blocks):
         for kb in range(pat.shape[1]):
             here = dens[b * size:(b + 1) * size, kb * size:(kb + 1) * size]
             keep = jnp.broadcast_to(pat[b:b + 1, kb:kb + 1], here.shape) != 0
             kept = jnp.where(keep, here.astype(jnp.float32), 0.0).astype(here.dtype)
-            rowb[z, x, b * size:(b + 1) * size, kb * size:(kb + 1) * size] = kept
+            rowb[z, pl.ds(x0 + b * size, size), kb * size:(kb + 1) * size] = kept
             gb[0, pl.ds(c0 + b * size, size), kb * size:(kb + 1) * size] = kept
 
     def remote(src, dst, send, recv, device):
@@ -82,7 +90,7 @@
         )
 
     def row_copy(zz, xx, n, send, device):
-        ref = rowb.at[zz, xx, rows_at(n)]
+        ref = rowb.at[zz, rows_at(xx, n)]
         return remote(ref, ref, send, r_row.at[zz, xx, n], device)
 
     def up(zz, n):
@@ -91,8 +99,8 @@
     def down(zz, n):
         return row_copy(zz, x, n, s_dn.at[zz, n], dev_z(z - 1))
 
-    def double(n):
-        return row_copy(z, 1 - x, n, s_dup.at[n], dev_z(inward))
+    def double(zz, n):
+        return row_copy(zz, 1 - x, n, s_dup.at[n], dev_z(inward))
 
     def across(zz, n):
         return row_copy(zz, x, n, s_x.at[zz, n], dev_x)
@@ -101,13 +109,13 @@
         return remote(src, gb.at[p, gb_rows(cc, n)], send, r_gb.at[p, cc, n], device)
 
     def sideways(p, d, n):
-        src = gb.at[0, gb_rows(c, n)] if p == 0 else rowb.at[ze, x, rows_at(n)]
+        src = gb.at[0, gb_rows(c, n)] if p == 0 else rowb.at[ze, rows_at(x, n)]
         return gb_send(p, src, c, n, s_y.at[p, d, n], dev_y(d))
 
     def to_twin(p, d, n):
         cc = lax.rem(y + d, yn) * 2 + k
         if p == 1 and d == 0:
-            src = rowb.at[ze, x, rows_at(n)]
+            src = rowb.at[ze, rows_at(x, n)]
         else:
             src = gb.at[p, gb_rows(cc, n)]
         return gb_send(p, src, cc, n, s_c.at[p, d, n], dev_k)
@@ -119,9 +127,11 @@
         ref = gb.at[p, gb_rows(cc, n)]
         remote(ref, ref, s_dup.at[n], r_gb.at[p, cc, n], dev_x).wait_recv()
 
-    def own_sends(n, do):
+    def own_sideways(n, do):
         for d in range(1, yn):
             do(sideways(0, d, n))
+
+    def own_sends(n, do):
         do(across(z, n))
         when(z < zn - 1, lambda: do(up(z, n)))
         when(z > 0, lambda: do(down(z, n)))
@@ -142,11 +152,16 @@
         def _():
             do(down(zz, n))
 
+        dist = jnp.abs(zz - z)
+        twice = ((zz == 0) | (zz == zn - 1)) & (
+            (dist == 1) | ((dist == 2) & (n >= HALF))
+        )
+
+        @pl.when(jnp.logical_not(twice))
+        def _():
+            do(across(zz, n))
+
         adjacent = proxy & (zz == ze)
-
-        @pl.when(jnp.logical_not(adjacent))
-        def _():
-            do(across(zz, n))
 
         @pl.when(adjacent)
         def _():
@@ -163,21 +178,18 @@
     def finish(copy):
         copy.wait_send()
 
-    step_rows = min(group, 512)
-
-    def product(p, zz, xx, target, slot):
+    step_rows = min(group, 256)
+
+    def product(p, panel, store):
         def body(i, carry):
             at = pl.ds(pl.multiple_of(i * step_rows, step_rows), step_rows)
-            target[slot, at, :] = lax.dot_general(
-                gb[p, at, :], rowb[zz, xx], (((1,), (1,)), ((), ())),
+            store(at, lax.dot_general(
+                gb[p, at, :], panel[...], (((1,), (1,)), ((), ())),
                 preferred_element_type=jnp.float32,
-            ).astype(target.dtype)
+            ).astype(ob.dtype))
             return carry
 
-        if group == step_rows:
-            body(0, 0)
-        else:
-            lax.fori_loop(0, group // step_rows, body, 0)
+        lax.fori_loop(0, group // step_rows, body, 0)
 
     def slot_of(gg, q):
         return lax.rem(gg + half_span - q + rows_n, rows_n)
@@ -185,10 +197,16 @@
     def out_copy(s):
         return pltpu.make_async_copy(ob.at[s], out.at[s], s_out.at[s])
 
-    def own_job(zz, xx):
-        s = slot_of(g, row_of(zz, xx))
-        product(0, zz, xx, ob, s)
-        out_copy(s).start()
+    def own_job(zz):
+        slots = [slot_of(g, row_of(zz, xx)) for xx in range(2)]
+
+        def store(at, value):
+            for xx in range(2):
+                ob[slots[xx], at, :] = value[:, xx * length:(xx + 1) * length]
+
+        product(0, rowb.at[zz], store)
+        for xx in range(2):
+            out_copy(slots[xx]).start()
 
     def proxy_copy(q):
         s = slot_of(row_of(ze, x), q)
@@ -196,7 +214,11 @@
 
     def proxy_job(zz, xx):
         q = row_of(zz, xx)
-        product(1, zz, xx, pb, q)
+
+        def store(at, value):
+            pb[q, at, :] = value
+
+        product(1, rowb.at[zz, pl.ds(pl.multiple_of(xx * length, length), length)], store)
         proxy_copy(q).start()
 
     def all_twin(p):
@@ -209,30 +231,31 @@
 
     for n in range(CHUNKS):
         own_sends(n, start)
+
+        @pl.when(edge | (n < HALF))
+        def _():
+            own_sideways(n, start)
 
     @pl.when(edge)
     def _():
         for n in range(CHUNKS):
             y_arrivals(0, n, start, True)
             got_row(z, 1 - x, n)
-            double(n).start()
+            double(z, n).start()
             got_row(inward, x, n)
             across(inward, n).start()
         all_twin(0)
 
         def job(j, carry):
-            zz = jnp.where(j < 2, z, inward)
-            xx = jnp.where(lax.rem(j, 2) == 0, x, 1 - x)
-
-            @pl.when(j == 3)
+            @pl.when(j == 1)
             def _():
                 for n in range(CHUNKS):
                     got_row(inward, 1 - x, n)
 
-            own_job(zz, xx)
+            own_job(jnp.where(j == 0, z, inward))
             return carry
 
-        lax.fori_loop(0, 4, job, 0)
+        lax.fori_loop(0, 2, job, 0)
 
         def far(i, carry):
             zz = inward + away * (i // 2 + 1)
@@ -247,70 +270,116 @@
     @pl.when(inner)
     def _():
         def turn(t, carry):
-            for n in range(CHUNKS):
-                @pl.when(t == 1)
-                def _():
-                    y_arrivals(0, n, start, True)
-
-                @pl.when((t == 2) & proxy)
-                def _():
-                    y_arrivals(1, n, start, True)
-
+            first, second = t == 1, t == 2
+
+            def forwards(n):
                 for zz in (z - t * away, z + t * away):
                     @pl.when(inside(zz))
                     def _():
                         got_row(zz, x, n)
                         relay(zz, n, start)
 
-            @pl.when(t == 1)
+                @pl.when(second & proxy)
+                def _():
+                    got_row(ze, 1 - x, n)
+                    if n >= HALF:
+                        double(ze, n).start()
+
+            def sides(early, late):
+                @pl.when(first)
+                def _():
+                    for n in early:
+                        y_arrivals(0, n, start, True)
+
+                @pl.when(second)
+                def _():
+                    for n in late:
+                        y_arrivals(0, n, start, True)
+
+            def proxied(dist, xx):
+                @pl.when(proxy & (dist >= 1) & inside(z + dist * away))
+                def _():
+                    proxy_job(z + dist * away, xx)
+
+            for n in range(HALF):
+                forwards(n)
+                sides([n], [])
+
+            @pl.when(second & proxy)
+            def _():
+                for n in range(CHUNKS):
+                    y_arrivals(1, n, start, True)
+                all_twin(1)
+                proxied(t - 1, x)
+
+            for n in range(HALF, CHUNKS):
+                forwards(n)
+                sides([], [n])
+
+            @pl.when(first)
+            def _():
+                for n in range(HALF, CHUNKS):
+                    own_sideways(n, start)
+
+            @pl.when(first & proxy)
+            def _():
+                gb[1, pl.ds(c0, length), :] = rowb[ze, pl.ds(x0, length), :]
+
+            @pl.when(second)
+            def _():
+                for n in range(CHUNKS):
+                    got_row(z, 1 - x, n)
+
+            def job(j, inner_carry):
+                dist = jnp.where(j == 0, t - 1, t)
+                xx = jnp.where(j == 0, 1 - x, x)
+
+                @pl.when(j == 0)
+                def _():
+                    for zz in (z - (t - 1) * away, z + (t - 1) * away):
+                        @pl.when(inside(zz) & jnp.logical_not(proxy & (zz == ze)))
+                        def _():
+                            for n in range(CHUNKS):
+                                got_row(zz, 1 - x, n)
+
+                proxied(dist, xx)
+                return inner_carry
+
+            @pl.when(t > 1)
+            def _():
+                lax.fori_loop(0, 2, job, 0)
+
+            @pl.when(second)
             def _():
                 all_twin(0)
 
-            @pl.when((t == 2) & proxy)
-            def _():
-                gb[1, pl.ds(c0, length), :] = rowb[ze, x]
-                all_twin(1)
-
-            def job(j, inner_carry):
-                dist = jnp.where(j < 3, t - 1, t)
-                sign = jnp.where((j == 2) | (j == 4), -away, away)
-                zz = z + sign * dist
-                other = (j == 1) | (j == 2)
-                xx = jnp.where(other, 1 - x, x)
-                valid = inside(zz) & jnp.where(
-                    j == 0, t <= 2, jnp.where(j == 2, t >= 2, True)
-                )
-
-                @pl.when(valid & other)
-                def _():
-                    for n in range(CHUNKS):
-                        got_row(zz, 1 - x, n)
-
-                @pl.when(
-                    valid & proxy & (t >= 2) & ((j == 0) | (j == 1) | (j == 3))
-                )
-                def _():
-                    proxy_job(zz, xx)
-
-                @pl.when(valid & jnp.where(j == 0, t == 1, True))
-                def _():
-                    own_job(zz, xx)
+            def own(j, inner_carry):
+                dist = jnp.where(j == 0, 0, t - 1)
+                zz = z + jnp.where(j == 1, -dist, dist) * away
+
+                @pl.when(inside(zz) & ((j > 0) | second))
+                def _():
+                    own_job(zz)
 
                 return inner_carry
 
-            lax.fori_loop(0, 5, job, 0)
+            @pl.when(t > 1)
+            def _():
+                lax.fori_loop(0, 3, own, 0)
+
             return carry
 
         lax.fori_loop(1, zn, turn, 0)
 
     for n in range(CHUNKS):
         own_sends(n, finish)
+        own_sideways(n, finish)
         y_arrivals(0, n, finish, False)
 
     @pl.when(edge)
     def _():
         for n in range(CHUNKS):
-            double(n).wait_send()
+            double(z, n).wait_send()
             across(inward, n).wait_send()
 
     @pl.when(inner)
@@ -319,6 +388,8 @@
         def _():
             for n in range(CHUNKS):
                 y_arrivals(1, n, finish, False)
+            for n in range(HALF, CHUNKS):
+                double(ze, n).wait_send()
 
             def sent(i, carry):
                 zz = z + away * (i // 2 + 1)
@@ -355,13 +426,16 @@
     out = pl.pallas_call(
         functools.partial(kernel, rows_n, cols_n),
         out_shape=jax.ShapeDtypeStruct((rows_n, group, length), kind),
-        in_specs=[pl.BlockSpec(memory_space=pltpu.VMEM)] * 2,
+        in_specs=[pl.BlockSpec(memory_space=pltpu.HBM)] * 2,
         out_specs=pl.BlockSpec(memory_space=pl.ANY),
         scratch_shapes=[
-            pltpu.VMEM((zn, 2, length, width), kind),
+            pltpu.VMEM((length, width), kind),
+            pltpu.VMEM(pattern.shape, pattern.dtype),
+            pltpu.VMEM((zn, 2 * length, width), kind),
             pltpu.VMEM((2, group, width), kind),
             pltpu.VMEM((rows_n, group, length), kind),
             pltpu.VMEM((rows_n, group, length), kind),
+            dma((2,)),
             dma((zn, 2, CHUNKS)),
             dma((2, cols_n, CHUNKS)),
             dma((rows_n,)),
@@ -375,7 +449,7 @@
             dma((rows_n,)),
         ],
         compiler_params=pltpu.CompilerParams(
-            collective_id=0, has_side_effects=True, vmem_limit_bytes=2 * words + (8 << 20)
+            collective_id=0, has_side_effects=True, vmem_limit_bytes=max(2 * words + (8 << 20), 56 << 20)
         ),
         cost_estimate=pl.CostEstimate(
             flops=2 * group * length * width * rows_n,

time: 41.3 us -> 39.2 us (0.949)
  Pallas kernels: 37.8 us -> 36.1 us
  local copies, waits for them, and re-layouts: 3.3 us -> 2.87 us
    pallas_call x1, Pallas kernels: 37.8 us -> 36.1 us  [local(): pl.pallas_call(functools.partial(kernel, rows_n, cols_n), out_shape=jax.S...]
    unnamed x4 -> x0, local copies, waits for them, and re-layouts: 1.65 us -> none
    transpose x1, local copies, waits for them, and re-layouts: 1.65 us -> 2.87 us  [local(): return jnp.transpose(out, (1, 0, 2))]
where the time goes in v2:
time: 39.2 us; the launch traced here: 39 us
  Pallas kernels  36.1 us (92%)
  local copies, waits for them, and re-layouts  2.87 us (7%)
    pallas_call x1, Pallas kernels, local(): pl.pallas_call(functools.partial(kernel, rows_n, cols_n), out_shape=jax.S...  36.1 us
    transpose x1, local copies, waits for them, and re-layouts, local(): return jnp.transpose(out, (1, 0, 2))  2.87 us

profile of v2, /device:TPU:0, one launch (start us, length us, event | category | flops | bytes accessed | tf_op | source)
XLA Modules:
  0.0 39.0 jit_solution(7288651427841876471)
XLA Ops:
  0.0 36.1 %shard_map.28 = bf16[8,512,128]{2,1,0:T(8,128)(2,1)} custom-call(bf16[128,1536]{1,0:T(8,128)(2,1)} %dens_hbm.1, s32[1,12]{1,0:T(1,128)} %pat_hbm.1), custom_call_target="tpu_custom_call" | custom-call | flops 1610612736 | bytes 1048576 | tf_op jit(solution)/shard_map/pallas_call | solution.py:426
  36.1 2.9 %copy.3 = bf16[512,8,128]{2,1,0:T(8,128)(2,1)} copy(bf16[512,8,128]{2,0,1:T(8,128)(2,1)} %bitcast.1) | data formatting | bytes 2097152 | tf_op jit(solution)/shard_map/transpose | solution.py:460

commit v3 on v2

--- a/solution.py
+++ b/solution.py
@@ -10,11 +10,12 @@
 MESH = pl.DeviceIdType.MESH
 CHUNKS = 4
 HALF = CHUNKS // 2
+LAST = CHUNKS - 1
 
 
 def kernel(
-    rows_n, cols_n, dens_hbm, pat_hbm, out, dens, pat, rowb, gb, ob, pb, s_in,
-    r_row, r_gb, r_ob, s_up, s_dn, s_dup, s_x, s_y, s_c, s_p, s_out,
+    rows_n, cols_n, dens_hbm, pat_hbm, ob, dens, pat, rowb, gb, pb, s_in,
+    r_row, r_gb, r_ob, s_up, s_dn, s_dup, s_x, s_y, s_c, s_p,
 ):
     fetch_dens = pltpu.make_async_copy(dens_hbm, dens, s_in.at[0])
     fetch_pat = pltpu.make_async_copy(pat_hbm, pat, s_in.at[1])
@@ -100,7 +101,7 @@
         return row_copy(zz, x, n, s_dn.at[zz, n], dev_z(z - 1))
 
     def double(zz, n):
-        return row_copy(zz, 1 - x, n, s_dup.at[n], dev_z(inward))
+        return row_copy(zz, 1 - x, n, s_dup.at[jnp.where(zz == z, 0, 1), n], dev_z(inward))
 
     def across(zz, n):
         return row_copy(zz, x, n, s_x.at[zz, n], dev_x)
@@ -121,18 +122,21 @@
         return gb_send(p, src, cc, n, s_c.at[p, d, n], dev_k)
 
     def got_row(zz, xx, n):
-        row_copy(zz, xx, n, s_dup.at[n], dev_x).wait_recv()
+        row_copy(zz, xx, n, s_dup.at[0, n], dev_x).wait_recv()
 
     def got_gb(p, cc, n):
         ref = gb.at[p, gb_rows(cc, n)]
-        remote(ref, ref, s_dup.at[n], r_gb.at[p, cc, n], dev_x).wait_recv()
+        remote(ref, ref, s_dup.at[0, n], r_gb.at[p, cc, n], dev_x).wait_recv()
 
     def own_sideways(n, do):
         for d in range(1, yn):
             do(sideways(0, d, n))
 
     def own_sends(n, do):
-        do(across(z, n))
+        if n < HALF:
+            do(across(z, n))
+        else:
+            when(jnp.logical_not(proxy), lambda: do(across(z, n)))
         when(z < zn - 1, lambda: do(up(z, n)))
         when(z > 0, lambda: do(down(z, n)))
         do(to_twin(0, 0, n))
@@ -154,7 +158,7 @@
 
         dist = jnp.abs(zz - z)
         twice = ((zz == 0) | (zz == zn - 1)) & (
-            (dist == 1) | ((dist == 2) & (n >= HALF))
+            (dist == 1) | ((dist == 2) & (n >= LAST))
         )
 
         @pl.when(jnp.logical_not(twice))
@@ -194,9 +198,6 @@
     def slot_of(gg, q):
         return lax.rem(gg + half_span - q + rows_n, rows_n)
 
-    def out_copy(s):
-        return pltpu.make_async_copy(ob.at[s], out.at[s], s_out.at[s])
-
     def own_job(zz):
         slots = [slot_of(g, row_of(zz, xx)) for xx in range(2)]
 
@@ -205,8 +206,6 @@
                 ob[slots[xx], at, :] = value[:, xx * length:(xx + 1) * length]
 
         product(0, rowb.at[zz], store)
-        for xx in range(2):
-            out_copy(slots[xx]).start()
 
     def proxy_copy(q):
         s = slot_of(row_of(ze, x), q)
@@ -251,6 +250,8 @@
             def _():
                 for n in range(CHUNKS):
                     got_row(inward, 1 - x, n)
+                    if n >= HALF:
+                        double(inward, n).start()
 
             own_job(jnp.where(j == 0, z, inward))
             return carry
@@ -262,7 +263,6 @@
             xx = jnp.where(lax.rem(i, 2) == 0, x, 1 - x)
             s = slot_of(g, row_of(zz, xx))
             remote(ob.at[s], ob.at[s], s_p.at[0], r_ob.at[s], dev_x).wait_recv()
-            out_copy(s).start()
             return carry
 
         lax.fori_loop(0, 2 * (zn - 2), far, 0)
@@ -282,7 +282,7 @@
                 @pl.when(second & proxy)
                 def _():
                     got_row(ze, 1 - x, n)
-                    if n >= HALF:
+                    if n >= LAST:
                         double(ze, n).start()
 
             def sides(early, late):
@@ -300,6 +300,12 @@
                 @pl.when(proxy & (dist >= 1) & inside(z + dist * away))
                 def _():
                     proxy_job(z + dist * away, xx)
+
+            def got_other(zz):
+                @pl.when(inside(zz) & jnp.logical_not(proxy & (zz == ze)))
+                def _():
+                    for n in range(CHUNKS):
+                        got_row(zz, 1 - x, n)
 
             for n in range(HALF):
                 forwards(n)
@@ -313,6 +319,11 @@
                 proxied(t - 1, x)
 
             for n in range(HALF, CHUNKS):
+                if n == LAST:
+                    @pl.when(t > 1)
+                    def _():
+                        got_other(z + (t - 1) * away)
+                        proxied(t - 1, 1 - x)
                 forwards(n)
                 sides([], [n])
 
@@ -325,39 +336,25 @@
             def _():
                 gb[1, pl.ds(c0, length), :] = rowb[ze, pl.ds(x0, length), :]
 
+            @pl.when(t > 1)
+            def _():
+                proxied(t, x)
+                got_other(z - (t - 1) * away)
+
             @pl.when(second)
             def _():
-                for n in range(CHUNKS):
-                    got_row(z, 1 - x, n)
-
-            def job(j, inner_carry):
-                dist = jnp.where(j == 0, t - 1, t)
-                xx = jnp.where(j == 0, 1 - x, x)
-
-                @pl.when(j == 0)
-                def _():
-                    for zz in (z - (t - 1) * away, z + (t - 1) * away):
-                        @pl.when(inside(zz) & jnp.logical_not(proxy & (zz == ze)))
-                        def _():
-                            for n in range(CHUNKS):
-                                got_row(zz, 1 - x, n)
-
-                proxied(dist, xx)
-                return inner_carry
-
-            @pl.when(t > 1)
-            def _():
-                lax.fori_loop(0, 2, job, 0)
-
-            @pl.when(second)
-            def _():
                 all_twin(0)
 
             def own(j, inner_carry):
-                dist = jnp.where(j == 0, 0, t - 1)
-                zz = z + jnp.where(j == 1, -dist, dist) * away
-
-                @pl.when(inside(zz) & ((j > 0) | second))
+                zz = z + jnp.where(j == 0, 1 - t, jnp.where(j == 1, t - 1, 0)) * away
+                last = j == 2
+
+                @pl.when(last & (t == zn - 1))
+                def _():
+                    for n in range(CHUNKS):
+                        got_row(z, 1 - x, n)
+
+                @pl.when(inside(zz) & (jnp.logical_not(last) | (t == zn - 1)))
                 def _():
                     own_job(zz)
 
@@ -381,6 +378,8 @@
         for n in range(CHUNKS):
             double(z, n).wait_send()
             across(inward, n).wait_send()
+            if n >= HALF:
+                double(inward, n).wait_send()
 
     @pl.when(inner)
     def _():
@@ -388,7 +387,7 @@
         def _():
             for n in range(CHUNKS):
                 y_arrivals(1, n, finish, False)
-            for n in range(HALF, CHUNKS):
+            for n in range(LAST, CHUNKS):
                 double(ze, n).wait_send()
 
             def sent(i, carry):
@@ -407,12 +406,6 @@
             return carry
 
         lax.fori_loop(0, zn, relayed, 0)
-
-    def stored(s, carry):
-        out_copy(s).wait()
-        return carry
-
-    lax.fori_loop(0, rows_n, stored, 0)
 
 
 def local(density, pattern):
@@ -427,13 +420,12 @@
         functools.partial(kernel, rows_n, cols_n),
         out_shape=jax.ShapeDtypeStruct((rows_n, group, length), kind),
         in_specs=[pl.BlockSpec(memory_space=pltpu.HBM)] * 2,
-        out_specs=pl.BlockSpec(memory_space=pl.ANY),
+        out_specs=pl.BlockSpec(memory_space=pltpu.VMEM),
         scratch_shapes=[
             pltpu.VMEM((length, width), kind),
             pltpu.VMEM(pattern.shape, pattern.dtype),
             pltpu.VMEM((zn, 2 * length, width), kind),
             pltpu.VMEM((2, group, width), kind),
-            pltpu.VMEM((rows_n, group, length), kind),
             pltpu.VMEM((rows_n, group, length), kind),
             dma((2,)),
             dma((zn, 2, CHUNKS)),
@@ -441,22 +433,21 @@
             dma((rows_n,)),
             dma((zn, CHUNKS)),
             dma((zn, CHUNKS)),
-            dma((CHUNKS,)),
+            dma((2, CHUNKS)),
             dma((zn, CHUNKS)),
             dma((2, yn, CHUNKS)),
             dma((2, yn, CHUNKS)),
             dma((rows_n,)),
-            dma((rows_n,)),
         ],
         compiler_params=pltpu.CompilerParams(
-            collective_id=0, has_side_effects=True, vmem_limit_bytes=max(2 * words + (8 << 20), 56 << 20)
+            collective_id=0, has_side_effects=True, vmem_limit_bytes=2 * words + (8 << 20)
         ),
         cost_estimate=pl.CostEstimate(
             flops=2 * group * length * width * rows_n,
             bytes_accessed=2 * rows_n * group * length,
             transcendentals=0,
         ),
-    )(density, pattern)
+    )(*(pltpu.with_memory_space_constraint(a, pltpu.HBM) for a in (density, pattern)))
     return jnp.transpose(out, (1, 0, 2))
 
 

time: 39.2 us -> 37.3 us (0.952)
  local copies, waits for them, and re-layouts: 2.87 us -> 1.65 us
  Pallas kernels: 36.1 us -> 35.5 us
    transpose x1, local copies, waits for them, and re-layouts: 2.87 us -> 1.65 us  [local(): return jnp.transpose(out, (1, 0, 2))]
    pallas_call x1, Pallas kernels: 36.1 us -> 35.5 us  [local(): pl.pallas_call(functools.partial(kernel, rows_n, cols_n), out_shape=jax.S...]
where the time goes in v3:
time: 37.3 us; the launch traced here: 37.1 us
  Pallas kernels  35.5 us (95%)
  local copies, waits for them, and re-layouts  1.65 us (4%)
    pallas_call x1, Pallas kernels, local(): pl.pallas_call(functools.partial(kernel, rows_n, cols_n), out_shape=jax.S...  35.5 us
    transpose x1, local copies, waits for them, and re-layouts, local(): return jnp.transpose(out, (1, 0, 2))  1.65 us

profile of v3, /device:TPU:0, one launch (start us, length us, event | category | flops | bytes accessed | tf_op | source)
XLA Modules:
  0.0 37.1 jit_solution(7704914918297724556)
XLA Ops:
  0.0 35.5 %shard_map.28 = bf16[8,512,128]{2,1,0:T(8,128)(2,1)S(1)} custom-call(bf16[128,1536]{1,0:T(8,128)(2,1)} %dens_hbm.1, s32[1,12]{1,0:T(1,128)} %pat_hbm.1), custom_call_target="tpu_custom_call" | custom-call | flops 1610612736 | bytes 1048576 | tf_op jit(solution)/shard_map/pallas_call | solution.py:419
  35.5 1.6 %copy.3 = bf16[512,8,128]{2,1,0:T(8,128)(2,1)} copy(bf16[512,8,128]{2,0,1:T(8,128)(2,1)S(1)} %bitcast.1) | data formatting | bytes 2097152 | tf_op jit(solution)/shard_map/transpose | solution.py:451

commit v4 on v3

--- a/solution.py
+++ b/solution.py
@@ -15,7 +15,7 @@
 
 def kernel(
     rows_n, cols_n, dens_hbm, pat_hbm, ob, dens, pat, rowb, gb, pb, s_in,
-    r_row, r_gb, r_ob, s_up, s_dn, s_dup, s_x, s_y, s_c, s_p,
+    r_row, r_gb, r_tw, r_ob, s_up, s_dn, s_dup, s_x, s_y, s_c, s_p,
 ):
     fetch_dens = pltpu.make_async_copy(dens_hbm, dens, s_in.at[0])
     fetch_pat = pltpu.make_async_copy(pat_hbm, pat, s_in.at[1])
@@ -67,8 +67,13 @@
     def rows_at(xx, n):
         return pl.ds(pl.multiple_of(xx * length + n * part, part), part)
 
-    def gb_rows(cc, n):
-        return pl.ds(pl.multiple_of(cc * length + n * part, part), part)
+    side = length // 2
+
+    def gb_half(cc, h):
+        return pl.ds(pl.multiple_of(cc * length + h * side, side), side)
+
+    def gb_panel(cc):
+        return pl.ds(pl.multiple_of(cc * length, length), length)
 
     blocks = pat.shape[0]
     size = length // blocks
@@ -106,31 +111,39 @@
     def across(zz, n):
         return row_copy(zz, x, n, s_x.at[zz, n], dev_x)
 
-    def gb_send(p, src, cc, n, send, device):
-        return remote(src, gb.at[p, gb_rows(cc, n)], send, r_gb.at[p, cc, n], device)
-
-    def sideways(p, d, n):
-        src = gb.at[0, gb_rows(c, n)] if p == 0 else rowb.at[ze, rows_at(x, n)]
-        return gb_send(p, src, c, n, s_y.at[p, d, n], dev_y(d))
-
-    def to_twin(p, d, n):
+    def sideways(p, d, h):
+        if p == 0:
+            src = gb.at[0, gb_half(c, h)]
+        else:
+            src = rowb.at[ze, pl.ds(pl.multiple_of(x * length + h * side, side), side)]
+        return remote(
+            src, gb.at[p, gb_half(c, h)], s_y.at[p, d, h], r_gb.at[p, c, h], dev_y(d)
+        )
+
+    def to_twin(p, d):
         cc = lax.rem(y + d, yn) * 2 + k
         if p == 1 and d == 0:
-            src = rowb.at[ze, rows_at(x, n)]
+            src = rowb.at[ze, pl.ds(x0, length)]
         else:
-            src = gb.at[p, gb_rows(cc, n)]
-        return gb_send(p, src, cc, n, s_c.at[p, d, n], dev_k)
+            src = gb.at[p, gb_panel(cc)]
+        return remote(src, gb.at[p, gb_panel(cc)], s_c.at[p, d], r_tw.at[p, cc], dev_k)
 
     def got_row(zz, xx, n):
         row_copy(zz, xx, n, s_dup.at[0, n], dev_x).wait_recv()
 
-    def got_gb(p, cc, n):
-        ref = gb.at[p, gb_rows(cc, n)]
-        remote(ref, ref, s_dup.at[0, n], r_gb.at[p, cc, n], dev_x).wait_recv()
-
-    def own_sideways(n, do):
+    def got_side(p, d, h):
+        cc = lax.rem(y + d, yn) * 2 + k
+        ref = gb.at[p, gb_half(cc, h)]
+        remote(ref, ref, s_dup.at[0, 0], r_gb.at[p, cc, h], dev_x).wait_recv()
+
+    def got_twin(p, d):
+        cc = lax.rem(y + d, yn) * 2 + 1 - k
+        ref = gb.at[p, gb_panel(cc)]
+        remote(ref, ref, s_dup.at[0, 0], r_tw.at[p, cc], dev_x).wait_recv()
+
+    def own_sideways(h, do):
         for d in range(1, yn):
-            do(sideways(0, d, n))
+            do(sideways(0, d, h))
 
     def own_sends(n, do):
         if n < HALF:
@@ -139,13 +152,15 @@
             when(jnp.logical_not(proxy), lambda: do(across(z, n)))
         when(z < zn - 1, lambda: do(up(z, n)))
         when(z > 0, lambda: do(down(z, n)))
-        do(to_twin(0, 0, n))
-
-    def y_arrivals(p, n, do, wait):
+        if n == CHUNKS - 1:
+            do(to_twin(0, 0))
+
+    def y_arrivals(p, do, wait):
         for d in range(1, yn):
             if wait:
-                got_gb(p, lax.rem(y + d, yn) * 2 + k, n)
-            do(to_twin(p, d, n))
+                for h in range(2):
+                    got_side(p, d, h)
+            do(to_twin(p, d))
 
     def relay(zz, n, do):
         @pl.when((zz < z) & (z + 1 <= zn - 2))
@@ -169,9 +184,11 @@
 
         @pl.when(adjacent)
         def _():
-            for d in range(1, yn):
-                do(sideways(1, d, n))
-            do(to_twin(1, 0, n))
+            if n % HALF == HALF - 1:
+                for d in range(1, yn):
+                    do(sideways(1, d, n // HALF))
+            if n == CHUNKS - 1:
+                do(to_twin(1, 0))
 
     def inside(zz):
         return (zz >= 0) & (zz <= zn - 1)
@@ -182,18 +199,14 @@
     def finish(copy):
         copy.wait_send()
 
-    step_rows = min(group, 256)
-
-    def product(p, panel, store):
-        def body(i, carry):
-            at = pl.ds(pl.multiple_of(i * step_rows, step_rows), step_rows)
-            store(at, lax.dot_general(
-                gb[p, at, :], panel[...], (((1,), (1,)), ((), ())),
-                preferred_element_type=jnp.float32,
-            ).astype(ob.dtype))
-            return carry
-
-        lax.fori_loop(0, group // step_rows, body, 0)
+    step_rows = 2 * length
+
+    def product(p, block, panel, store):
+        at = pl.ds(pl.multiple_of(block * step_rows, step_rows), step_rows)
+        store(at, lax.dot_general(
+            gb[p, at, :], panel[...], (((1,), (1,)), ((), ())),
+            preferred_element_type=jnp.float32,
+        ).astype(ob.dtype))
 
     def slot_of(gg, q):
         return lax.rem(gg + half_span - q + rows_n, rows_n)
@@ -205,25 +218,33 @@
             for xx in range(2):
                 ob[slots[xx], at, :] = value[:, xx * length:(xx + 1) * length]
 
-        product(0, rowb.at[zz], store)
-
-    def proxy_copy(q):
+        def body(i, carry):
+            product(0, i, rowb.at[zz], store)
+            return carry
+
+        lax.fori_loop(0, yn, body, 0)
+
+    def proxy_copy(q, block):
         s = slot_of(row_of(ze, x), q)
-        return remote(pb.at[q], ob.at[s], s_p.at[q], r_ob.at[s], dev_z(ze))
-
-    def proxy_job(zz, xx):
+        at = pl.ds(pl.multiple_of(block * step_rows, step_rows), step_rows)
+        return remote(
+            pb.at[q, at], ob.at[s, at], s_p.at[q, block], r_ob.at[s, block], dev_z(ze)
+        )
+
+    def proxy_job(zz, xx, low_d, high_d):
         q = row_of(zz, xx)
 
         def store(at, value):
             pb[q, at, :] = value
 
-        product(1, rowb.at[zz, pl.ds(pl.multiple_of(xx * length, length), length)], store)
-        proxy_copy(q).start()
-
-    def all_twin(p):
-        for n in range(CHUNKS):
-            for d in range(yn):
-                got_gb(p, lax.rem(y + d, yn) * 2 + 1 - k, n)
+        def body(d, carry):
+            block = lax.rem(y + d, yn)
+            panel = rowb.at[zz, pl.ds(pl.multiple_of(xx * length, length), length)]
+            product(1, block, panel, store)
+            proxy_copy(q, block).start()
+            return carry
+
+        lax.fori_loop(low_d, high_d, body, 0)
 
     neighbours = 2 + (yn - 1)
     pl.semaphore_wait(barrier, neighbours + jnp.where(edge, 1, 2))
@@ -231,19 +252,21 @@
     for n in range(CHUNKS):
         own_sends(n, start)
 
-        @pl.when(edge | (n < HALF))
-        def _():
-            own_sideways(n, start)
+        if n == HALF - 1:
+            own_sideways(0, start)
+        if n == CHUNKS - 1:
+            when(edge, lambda: own_sideways(1, start))
 
     @pl.when(edge)
     def _():
         for n in range(CHUNKS):
-            y_arrivals(0, n, start, True)
             got_row(z, 1 - x, n)
             double(z, n).start()
             got_row(inward, x, n)
             across(inward, n).start()
-        all_twin(0)
+        y_arrivals(0, start, True)
+        for d in range(yn):
+            got_twin(0, d)
 
         def job(j, carry):
             @pl.when(j == 1)
@@ -258,19 +281,61 @@
 
         lax.fori_loop(0, 2, job, 0)
 
+        for n in range(CHUNKS):
+            own_sends(n, finish)
+            double(z, n).wait_send()
+            across(inward, n).wait_send()
+            if n >= HALF:
+                double(inward, n).wait_send()
+        own_sideways(0, finish)
+        own_sideways(1, finish)
+        y_arrivals(0, finish, False)
+
         def far(i, carry):
             zz = inward + away * (i // 2 + 1)
             xx = jnp.where(lax.rem(i, 2) == 0, x, 1 - x)
             s = slot_of(g, row_of(zz, xx))
-            remote(ob.at[s], ob.at[s], s_p.at[0], r_ob.at[s], dev_x).wait_recv()
+            for d in range(yn):
+                block = lax.rem(y + d, yn)
+                at = pl.ds(pl.multiple_of(block * step_rows, step_rows), step_rows)
+                ref = ob.at[s, at]
+                remote(ref, ref, s_p.at[0, 0], r_ob.at[s, block], dev_x).wait_recv()
             return carry
 
         lax.fori_loop(0, 2 * (zn - 2), far, 0)
 
     @pl.when(inner)
     def _():
+        def settle():
+            for n in range(CHUNKS):
+                own_sends(n, finish)
+            own_sideways(0, finish)
+            own_sideways(1, finish)
+            y_arrivals(0, finish, False)
+
+            @pl.when(proxy)
+            def _():
+                y_arrivals(1, finish, False)
+                for n in range(LAST, CHUNKS):
+                    double(ze, n).wait_send()
+
+            def relayed(zz, carry):
+                @pl.when(zz != z)
+                def _():
+                    for n in range(CHUNKS):
+                        relay(zz, n, finish)
+
+                return carry
+
+            lax.fori_loop(0, zn, relayed, 0)
+
         def turn(t, carry):
             first, second = t == 1, t == 2
+
+            @pl.when(t == zn - 1)
+            def _():
+                settle()
+
 
             def forwards(n):
                 for zz in (z - t * away, z + t * away):
@@ -285,21 +350,10 @@
                     if n >= LAST:
                         double(ze, n).start()
 
-            def sides(early, late):
-                @pl.when(first)
-                def _():
-                    for n in early:
-                        y_arrivals(0, n, start, True)
-
-                @pl.when(second)
-                def _():
-                    for n in late:
-                        y_arrivals(0, n, start, True)
-
-            def proxied(dist, xx):
+            def proxied(dist, xx, low_d=0, high_d=yn):
                 @pl.when(proxy & (dist >= 1) & inside(z + dist * away))
                 def _():
-                    proxy_job(z + dist * away, xx)
+                    proxy_job(z + dist * away, xx, low_d, high_d)
 
             def got_other(zz):
                 @pl.when(inside(zz) & jnp.logical_not(proxy & (zz == ze)))
@@ -309,14 +363,13 @@
 
             for n in range(HALF):
                 forwards(n)
-                sides([n], [])
 
             @pl.when(second & proxy)
             def _():
-                for n in range(CHUNKS):
-                    y_arrivals(1, n, start, True)
-                all_twin(1)
-                proxied(t - 1, x)
+                y_arrivals(1, start, True)
+                for d in range(1, yn):
+                    got_twin(1, d)
+                proxied(t - 1, x, 1)
 
             for n in range(HALF, CHUNKS):
                 if n == LAST:
@@ -325,16 +378,16 @@
                         got_other(z + (t - 1) * away)
                         proxied(t - 1, 1 - x)
                 forwards(n)
-                sides([], [n])
 
             @pl.when(first)
             def _():
-                for n in range(HALF, CHUNKS):
-                    own_sideways(n, start)
+                own_sideways(1, start)
 
             @pl.when(first & proxy)
             def _():
                 gb[1, pl.ds(c0, length), :] = rowb[ze, pl.ds(x0, length), :]
+                got_twin(1, 0)
+                proxied(t, x, 0, 1)
 
             @pl.when(t > 1)
             def _():
@@ -343,7 +396,9 @@
 
             @pl.when(second)
             def _():
-                all_twin(0)
+                y_arrivals(0, start, True)
+                for d in range(yn):
+                    got_twin(0, d)
 
             def own(j, inner_carry):
                 zz = z + jnp.where(j == 0, 1 - t, jnp.where(j == 1, t - 1, 0)) * away
@@ -368,44 +423,15 @@
 
         lax.fori_loop(1, zn, turn, 0)
 
-    for n in range(CHUNKS):
-        own_sends(n, finish)
-        own_sideways(n, finish)
-        y_arrivals(0, n, finish, False)
-
-    @pl.when(edge)
-    def _():
-        for n in range(CHUNKS):
-            double(z, n).wait_send()
-            across(inward, n).wait_send()
-            if n >= HALF:
-                double(inward, n).wait_send()
-
-    @pl.when(inner)
-    def _():
         @pl.when(proxy)
         def _():
-            for n in range(CHUNKS):
-                y_arrivals(1, n, finish, False)
-            for n in range(LAST, CHUNKS):
-                double(ze, n).wait_send()
-
             def sent(i, carry):
                 zz = z + away * (i // 2 + 1)
-                proxy_copy(row_of(zz, lax.rem(i, 2))).wait_send()
+                for d in range(yn):
+                    proxy_copy(row_of(zz, lax.rem(i, 2)), d).wait_send()
                 return carry
 
             lax.fori_loop(0, 2 * (zn - 2), sent, 0)
-
-        def relayed(zz, carry):
-            @pl.when(zz != z)
-            def _():
-                for n in range(CHUNKS):
-                    relay(zz, n, finish)
-
-            return carry
-
-        lax.fori_loop(0, zn, relayed, 0)
 
 
 def local(density, pattern):
@@ -429,15 +455,16 @@
             pltpu.VMEM((rows_n, group, length), kind),
             dma((2,)),
             dma((zn, 2, CHUNKS)),
-            dma((2, cols_n, CHUNKS)),
-            dma((rows_n,)),
+            dma((2, cols_n, 2)),
+            dma((2, cols_n)),
+            dma((rows_n, yn)),
             dma((zn, CHUNKS)),
             dma((zn, CHUNKS)),
             dma((2, CHUNKS)),
             dma((zn, CHUNKS)),
-            dma((2, yn, CHUNKS)),
-            dma((2, yn, CHUNKS)),
-            dma((rows_n,)),
+            dma((2, yn, 2)),
+            dma((2, yn)),
+            dma((rows_n, yn)),
         ],
         compiler_params=pltpu.CompilerParams(
             collective_id=0, has_side_effects=True, vmem_limit_bytes=2 * words + (8 << 20)

time: 37.3 us -> 37.2 us (level)
  no operation moved by 1% of the time
where the time goes in v4:
time: 37.2 us; the launch traced here: 37.1 us
  Pallas kernels  35.4 us (95%)
  local copies, waits for them, and re-layouts  1.65 us (4%)
    pallas_call x1, Pallas kernels, local(): pl.pallas_call(functools.partial(kernel, rows_n, cols_n), out_shape=jax.S...  35.4 us
    transpose x1, local copies, waits for them, and re-layouts, local(): return jnp.transpose(out, (1, 0, 2))  1.65 us

profile of v4, /device:TPU:0, one launch (start us, length us, event | category | flops | bytes accessed | tf_op | source)
XLA Modules:
  0.0 37.1 jit_solution(6281493557557956215)
XLA Ops:
  0.0 35.4 %shard_map.28 = bf16[8,512,128]{2,1,0:T(8,128)(2,1)S(1)} custom-call(bf16[128,1536]{1,0:T(8,128)(2,1)} %dens_hbm.1, s32[1,12]{1,0:T(1,128)} %pat_hbm.1), custom_call_target="tpu_custom_call" | custom-call | flops 1610612736 | bytes 1048576 | tf_op jit(solution)/shard_map/pallas_call | solution.py:445
  35.5 1.6 %copy.3 = bf16[512,8,128]{2,1,0:T(8,128)(2,1)} copy(bf16[512,8,128]{2,0,1:T(8,128)(2,1)S(1)} %bitcast.1) | data formatting | bytes 2097152 | tf_op jit(solution)/shard_map/transpose | solution.py:478

commit v5 on v4

--- a/solution.py
+++ b/solution.py
@@ -8,10 +8,11 @@
 from jax.sharding import PartitionSpec as P
 
 MESH = pl.DeviceIdType.MESH
-CHUNKS = 4
+CHUNKS = 8
 HALF = CHUNKS // 2
-LAST = CHUNKS - 1
-
+LAST = CHUNKS * 3 // 4
+EARLY = CHUNKS // 4
+LAG = 3
 
 def kernel(
     rows_n, cols_n, dens_hbm, pat_hbm, ob, dens, pat, rowb, gb, pb, s_in,
@@ -67,10 +68,8 @@
     def rows_at(xx, n):
         return pl.ds(pl.multiple_of(xx * length + n * part, part), part)
 
-    side = length // 2
-
-    def gb_half(cc, h):
-        return pl.ds(pl.multiple_of(cc * length + h * side, side), side)
+    def gb_rows(cc, n):
+        return pl.ds(pl.multiple_of(cc * length + n * part, part), part)
 
     def gb_panel(cc):
         return pl.ds(pl.multiple_of(cc * length, length), length)
@@ -111,39 +110,46 @@
     def across(zz, n):
         return row_copy(zz, x, n, s_x.at[zz, n], dev_x)
 
-    def sideways(p, d, h):
-        if p == 0:
-            src = gb.at[0, gb_half(c, h)]
-        else:
-            src = rowb.at[ze, pl.ds(pl.multiple_of(x * length + h * side, side), side)]
+    def sideways(p, d, n):
+        src = gb.at[0, gb_rows(c, n)] if p == 0 else rowb.at[ze, rows_at(x, n)]
         return remote(
-            src, gb.at[p, gb_half(c, h)], s_y.at[p, d, h], r_gb.at[p, c, h], dev_y(d)
+            src, gb.at[p, gb_rows(c, n)], s_y.at[p, d, n], r_gb.at[p, c, n], dev_y(d)
         )
 
-    def to_twin(p, d):
+    def to_twin(d):
         cc = lax.rem(y + d, yn) * 2 + k
-        if p == 1 and d == 0:
-            src = rowb.at[ze, pl.ds(x0, length)]
-        else:
-            src = gb.at[p, gb_panel(cc)]
-        return remote(src, gb.at[p, gb_panel(cc)], s_c.at[p, d], r_tw.at[p, cc], dev_k)
+        ref = gb.at[0, gb_panel(cc)]
+        return remote(ref, ref, s_c.at[0, d, 0], r_tw.at[0, cc, 0], dev_k)
+
+    def edge_to_twin(d, n):
+        cc = lax.rem(y + d, yn) * 2 + k
+        dst = gb.at[1, gb_rows(cc, n)]
+        src = rowb.at[ze, rows_at(x, n)] if d == 0 else dst
+        return remote(src, dst, s_c.at[1, d, n], r_tw.at[1, cc, n], dev_k)
 
     def got_row(zz, xx, n):
         row_copy(zz, xx, n, s_dup.at[0, n], dev_x).wait_recv()
 
-    def got_side(p, d, h):
+    def got_side(p, d, n):
         cc = lax.rem(y + d, yn) * 2 + k
-        ref = gb.at[p, gb_half(cc, h)]
-        remote(ref, ref, s_dup.at[0, 0], r_gb.at[p, cc, h], dev_x).wait_recv()
-
-    def got_twin(p, d):
+        ref = gb.at[p, gb_rows(cc, n)]
+        remote(ref, ref, s_dup.at[0, 0], r_gb.at[p, cc, n], dev_x).wait_recv()
+
+    def got_twin(d):
         cc = lax.rem(y + d, yn) * 2 + 1 - k
-        ref = gb.at[p, gb_panel(cc)]
-        remote(ref, ref, s_dup.at[0, 0], r_tw.at[p, cc], dev_x).wait_recv()
-
-    def own_sideways(h, do):
+        ref = gb.at[0, gb_panel(cc)]
+        remote(ref, ref, s_dup.at[0, 0], r_tw.at[0, cc, 0], dev_x).wait_recv()
+
+    def got_edge_twin(d):
+        cc = lax.rem(y + d, yn) * 2 + 1 - k
+        for n in range(CHUNKS):
+            ref = gb.at[1, gb_rows(cc, n)]
+            remote(ref, ref, s_dup.at[0, 0], r_tw.at[1, cc, n], dev_x).wait_recv()
+
+    def own_sideways(chunks, do):
         for d in range(1, yn):
-            do(sideways(0, d, h))
+            for n in chunks:
+                do(sideways(0, d, n))
 
     def own_sends(n, do):
         if n < HALF:
@@ -153,14 +159,20 @@
         when(z < zn - 1, lambda: do(up(z, n)))
         when(z > 0, lambda: do(down(z, n)))
         if n == CHUNKS - 1:
-            do(to_twin(0, 0))
-
-    def y_arrivals(p, do, wait):
+            do(to_twin(0))
+
+    def y_arrivals(do, wait):
         for d in range(1, yn):
             if wait:
-                for h in range(2):
-                    got_side(p, d, h)
-            do(to_twin(p, d))
+                for n in range(CHUNKS):
+                    got_side(0, d, n)
+            do(to_twin(d))
+
+    def edge_arrivals(n, do, wait):
+        for d in range(1, yn):
+            if wait:
+                got_side(1, d, n)
+            do(edge_to_twin(d, n))
 
     def relay(zz, n, do):
         @pl.when((zz < z) & (z + 1 <= zn - 2))
@@ -184,11 +196,9 @@
 
         @pl.when(adjacent)
         def _():
-            if n % HALF == HALF - 1:
-                for d in range(1, yn):
-                    do(sideways(1, d, n // HALF))
-            if n == CHUNKS - 1:
-                do(to_twin(1, 0))
+            for d in range(1, yn):
+                do(sideways(1, d, n))
+            do(edge_to_twin(0, n))
 
     def inside(zz):
         return (zz >= 0) & (zz <= zn - 1)
@@ -252,10 +262,10 @@
     for n in range(CHUNKS):
         own_sends(n, start)
 
-        if n == HALF - 1:
-            own_sideways(0, start)
-        if n == CHUNKS - 1:
-            when(edge, lambda: own_sideways(1, start))
+        if n < EARLY:
+            own_sideways([n], start)
+        else:
+            when(edge, functools.partial(own_sideways, [n], start))
 
     @pl.when(edge)
     def _():
@@ -264,9 +274,9 @@
             double(z, n).start()
             got_row(inward, x, n)
             across(inward, n).start()
-        y_arrivals(0, start, True)
+        y_arrivals(start, True)
         for d in range(yn):
-            got_twin(0, d)
+            got_twin(d)
 
         def job(j, carry):
             @pl.when(j == 1)
@@ -287,9 +297,8 @@
             across(inward, n).wait_send()
             if n >= HALF:
                 double(inward, n).wait_send()
-        own_sideways(0, finish)
-        own_sideways(1, finish)
-        y_arrivals(0, finish, False)
+        own_sideways(range(CHUNKS), finish)
+        y_arrivals(finish, False)
 
         def far(i, carry):
             zz = inward + away * (i // 2 + 1)
@@ -309,13 +318,13 @@
         def settle():
             for n in range(CHUNKS):
                 own_sends(n, finish)
-            own_sideways(0, finish)
-            own_sideways(1, finish)
-            y_arrivals(0, finish, False)
+            own_sideways(range(CHUNKS), finish)
+            y_arrivals(finish, False)
 
             @pl.when(proxy)
             def _():
-                y_arrivals(1, finish, False)
+                for n in range(CHUNKS):
+                    edge_arrivals(n, finish, False)
                 for n in range(LAST, CHUNKS):
                     double(ze, n).wait_send()
 
@@ -335,7 +344,6 @@
             @pl.when(t == zn - 1)
             def _():
                 settle()
-
 
             def forwards(n):
                 for zz in (z - t * away, z + t * away):
@@ -361,33 +369,32 @@
                     for n in range(CHUNKS):
                         got_row(zz, 1 - x, n)
 
-            for n in range(HALF):
-                forwards(n)
-
-            @pl.when(second & proxy)
-            def _():
-                y_arrivals(1, start, True)
-                for d in range(1, yn):
-                    got_twin(1, d)
-                proxied(t - 1, x, 1)
-
-            for n in range(HALF, CHUNKS):
-                if n == LAST:
+            for n in range(CHUNKS):
+                if n == HALF:
                     @pl.when(t > 1)
                     def _():
                         got_other(z + (t - 1) * away)
                         proxied(t - 1, 1 - x)
                 forwards(n)
+                if n >= LAG:
+                    @pl.when(first & proxy)
+                    def _():
+                        edge_arrivals(n - LAG, start, True)
 
             @pl.when(first)
             def _():
-                own_sideways(1, start)
+                own_sideways(range(EARLY, CHUNKS), start)
 
             @pl.when(first & proxy)
             def _():
                 gb[1, pl.ds(c0, length), :] = rowb[ze, pl.ds(x0, length), :]
-                got_twin(1, 0)
+                got_edge_twin(0)
                 proxied(t, x, 0, 1)
+                for n in range(CHUNKS - LAG, CHUNKS):
+                    edge_arrivals(n, start, True)
+                for d in range(1, yn):
+                    got_edge_twin(d)
+                proxied(t, x, 1)
 
             @pl.when(t > 1)
             def _():
@@ -396,9 +403,9 @@
 
             @pl.when(second)
             def _():
-                y_arrivals(0, start, True)
+                y_arrivals(start, True)
                 for d in range(yn):
-                    got_twin(0, d)
+                    got_twin(d)
 
             def own(j, inner_carry):
                 zz = z + jnp.where(j == 0, 1 - t, jnp.where(j == 1, t - 1, 0)) * away
@@ -455,15 +462,15 @@
             pltpu.VMEM((rows_n, group, length), kind),
             dma((2,)),
             dma((zn, 2, CHUNKS)),
-            dma((2, cols_n, 2)),
-            dma((2, cols_n)),
+            dma((2, cols_n, CHUNKS)),
+            dma((2, cols_n, CHUNKS)),
             dma((rows_n, yn)),
             dma((zn, CHUNKS)),
             dma((zn, CHUNKS)),
             dma((2, CHUNKS)),
             dma((zn, CHUNKS)),
-            dma((2, yn, 2)),
-            dma((2, yn)),
+            dma((2, yn, CHUNKS)),
+            dma((2, yn, CHUNKS)),
             dma((rows_n, yn)),
         ],
         compiler_params=pltpu.CompilerParams(

time: 37.2 us -> 38.3 us (1.030)
  Pallas kernels: 35.4 us -> 36.5 us
    pallas_call x1, Pallas kernels: 35.4 us -> 36.5 us  [local(): pl.pallas_call(functools.partial(kernel, rows_n, cols_n), out_shape=jax.S...]
where the time goes in v5:
time: 38.3 us; the launch traced here: 38.2 us
  Pallas kernels  36.5 us (95%)
  local copies, waits for them, and re-layouts  1.65 us (4%)
    pallas_call x1, Pallas kernels, local(): pl.pallas_call(functools.partial(kernel, rows_n, cols_n), out_shape=jax.S...  36.5 us
    transpose x1, local copies, waits for them, and re-layouts, local(): return jnp.transpose(out, (1, 0, 2))  1.65 us

profile of v5, /device:TPU:0, one launch (start us, length us, event | category | flops | bytes accessed | tf_op | source)
XLA Modules:
  0.0 38.2 jit_solution(12086911425824698292)
XLA Ops:
  0.0 36.5 %shard_map.28 = bf16[8,512,128]{2,1,0:T(8,128)(2,1)S(1)} custom-call(bf16[128,1536]{1,0:T(8,128)(2,1)} %dens_hbm.1, s32[1,12]{1,0:T(1,128)} %pat_hbm.1), custom_call_target="tpu_custom_call" | custom-call | flops 1610612736 | bytes 1048576 | tf_op jit(solution)/shard_map/pallas_call | solution.py:452
  36.5 1.6 %copy.3 = bf16[512,8,128]{2,1,0:T(8,128)(2,1)} copy(bf16[512,8,128]{2,0,1:T(8,128)(2,1)S(1)} %bitcast.1) | data formatting | bytes 2097152 | tf_op jit(solution)/shard_map/transpose | solution.py:485

commit v6 on v5

--- a/solution.py
+++ b/solution.py
@@ -8,11 +8,11 @@
 from jax.sharding import PartitionSpec as P
 
 MESH = pl.DeviceIdType.MESH
-CHUNKS = 8
+CHUNKS = 4
 HALF = CHUNKS // 2
 LAST = CHUNKS * 3 // 4
 EARLY = CHUNKS // 4
-LAG = 3
+LAG = 2
 
 def kernel(
     rows_n, cols_n, dens_hbm, pat_hbm, ob, dens, pat, rowb, gb, pb, s_in,

time: 38.3 us -> 37.6 us (0.982)
  Pallas kernels: 36.5 us -> 35.9 us
    pallas_call x1, Pallas kernels: 36.5 us -> 35.9 us  [local(): pl.pallas_call(functools.partial(kernel, rows_n, cols_n), out_shape=jax.S...]
where the time goes in v6:
time: 37.6 us; the launch traced here: 37.5 us
  Pallas kernels  35.9 us (95%)
  local copies, waits for them, and re-layouts  1.65 us (4%)
    pallas_call x1, Pallas kernels, local(): pl.pallas_call(functools.partial(kernel, rows_n, cols_n), out_shape=jax.S...  35.9 us
    transpose x1, local copies, waits for them, and re-layouts, local(): return jnp.transpose(out, (1, 0, 2))  1.65 us

profile of v6, /device:TPU:0, one launch (start us, length us, event | category | flops | bytes accessed | tf_op | source)
XLA Modules:
  0.0 37.5 jit_solution(3351239469477744650)
XLA Ops:
  0.0 35.9 %shard_map.28 = bf16[8,512,128]{2,1,0:T(8,128)(2,1)S(1)} custom-call(bf16[128,1536]{1,0:T(8,128)(2,1)} %dens_hbm.1, s32[1,12]{1,0:T(1,128)} %pat_hbm.1), custom_call_target="tpu_custom_call" | custom-call | flops 1610612736 | bytes 1048576 | tf_op jit(solution)/shard_map/pallas_call | solution.py:452
  35.9 1.6 %copy.3 = bf16[512,8,128]{2,1,0:T(8,128)(2,1)} copy(bf16[512,8,128]{2,0,1:T(8,128)(2,1)S(1)} %bitcast.1) | data formatting | bytes 2097152 | tf_op jit(solution)/shard_map/transpose | solution.py:485

commit v7 on v6

--- a/solution.py
+++ b/solution.py
@@ -13,6 +13,7 @@
 LAST = CHUNKS * 3 // 4
 EARLY = CHUNKS // 4
 LAG = 2
+WINDOW = 2
 
 def kernel(
     rows_n, cols_n, dens_hbm, pat_hbm, ob, dens, pat, rowb, gb, pb, s_in,
@@ -151,15 +152,19 @@
             for n in chunks:
                 do(sideways(0, d, n))
 
-    def own_sends(n, do):
+    def x_own(n, do):
         if n < HALF:
             do(across(z, n))
         else:
             when(jnp.logical_not(proxy), lambda: do(across(z, n)))
+
+    def z_own(n, do):
         when(z < zn - 1, lambda: do(up(z, n)))
         when(z > 0, lambda: do(down(z, n)))
-        if n == CHUNKS - 1:
-            do(to_twin(0))
+
+    def own_sends(n, do):
+        x_own(n, do)
+        z_own(n, do)
 
     def y_arrivals(do, wait):
         for d in range(1, yn):
@@ -174,15 +179,30 @@
                 got_side(1, d, n)
             do(edge_to_twin(d, n))
 
+    def relay_z(zz, n, do):
+        @pl.when(inside(zz) & (zz < z) & (z + 1 <= zn - 2))
+        def _():
+            do(up(zz, n))
+
+        @pl.when(inside(zz) & (zz > z) & (z - 1 >= 1))
+        def _():
+            do(down(zz, n))
+
+    def z_step(t, n):
+        ahead = n + WINDOW
+        dist, m = (t - 1, ahead) if ahead < CHUNKS else (t, ahead - CHUNKS)
+
+        @pl.when(dist == 0)
+        def _():
+            x_own(m, start)
+            z_own(m, start)
+
+        @pl.when(dist != 0)
+        def _():
+            relay_z(z - dist, m, start)
+            relay_z(z + dist, m, start)
+
     def relay(zz, n, do):
-        @pl.when((zz < z) & (z + 1 <= zn - 2))
-        def _():
-            do(up(zz, n))
-
-        @pl.when((zz > z) & (z - 1 >= 1))
-        def _():
-            do(down(zz, n))
-
         dist = jnp.abs(zz - z)
         twice = ((zz == 0) | (zz == zn - 1)) & (
             (dist == 1) | ((dist == 2) & (n >= LAST))
@@ -259,33 +279,37 @@
     neighbours = 2 + (yn - 1)
     pl.semaphore_wait(barrier, neighbours + jnp.where(edge, 1, 2))
 
-    for n in range(CHUNKS):
+    for n in range(WINDOW):
         own_sends(n, start)
-
-        if n < EARLY:
-            own_sideways([n], start)
-        else:
-            when(edge, functools.partial(own_sideways, [n], start))
+    own_sideways(range(EARLY), start)
+    to_twin(0).start()
 
     @pl.when(edge)
     def _():
+        turned = [(m + HALF) % CHUNKS for m in range(CHUNKS)]
+        own_sideways(range(EARLY, CHUNKS), start)
         for n in range(CHUNKS):
             got_row(z, 1 - x, n)
-            double(z, n).start()
             got_row(inward, x, n)
-            across(inward, n).start()
+            m = n + WINDOW
+            if m < CHUNKS:
+                own_sends(m, start)
+            else:
+                double(z, m - CHUNKS).start()
+                across(inward, turned[m - CHUNKS]).start()
         y_arrivals(start, True)
+        for n in range(CHUNKS):
+            got_row(inward, 1 - x, turned[n])
+            m = n + WINDOW
+            if m < CHUNKS:
+                double(z, m).start()
+                across(inward, turned[m]).start()
+            elif m - CHUNKS < CHUNKS - HALF:
+                double(inward, turned[m - CHUNKS]).start()
         for d in range(yn):
             got_twin(d)
 
         def job(j, carry):
-            @pl.when(j == 1)
-            def _():
-                for n in range(CHUNKS):
-                    got_row(inward, 1 - x, n)
-                    if n >= HALF:
-                        double(inward, n).start()
-
             own_job(jnp.where(j == 0, z, inward))
             return carry
 
@@ -298,6 +322,7 @@
             if n >= HALF:
                 double(inward, n).wait_send()
         own_sideways(range(CHUNKS), finish)
+        to_twin(0).wait_send()
         y_arrivals(finish, False)
 
         def far(i, carry):
@@ -319,6 +344,7 @@
             for n in range(CHUNKS):
                 own_sends(n, finish)
             own_sideways(range(CHUNKS), finish)
+            to_twin(0).wait_send()
             y_arrivals(finish, False)
 
             @pl.when(proxy)
@@ -333,6 +359,7 @@
                 def _():
                     for n in range(CHUNKS):
                         relay(zz, n, finish)
+                        relay_z(zz, n, finish)
 
                 return carry
 
@@ -376,14 +403,13 @@
                         got_other(z + (t - 1) * away)
                         proxied(t - 1, 1 - x)
                 forwards(n)
+                z_step(t, n)
+                if n + EARLY < CHUNKS:
+                    when(second, functools.partial(own_sideways, [n + EARLY], start))
                 if n >= LAG:
                     @pl.when(first & proxy)
                     def _():
                         edge_arrivals(n - LAG, start, True)
-
-            @pl.when(first)
-            def _():
-                own_sideways(range(EARLY, CHUNKS), start)
 
             @pl.when(first & proxy)
             def _():

time: 37.6 us -> 41 us (1.090)
  Pallas kernels: 35.9 us -> 39.2 us
    pallas_call x1, Pallas kernels: 35.9 us -> 39.2 us  [local(): pl.pallas_call(functools.partial(kernel, rows_n, cols_n), out_shape=jax.S...]
where the time goes in v7:
time: 41 us; the launch traced here: 40.9 us
  Pallas kernels  39.2 us (96%)
  local copies, waits for them, and re-layouts  1.65 us (4%)
    pallas_call x1, Pallas kernels, local(): pl.pallas_call(functools.partial(kernel, rows_n, cols_n), out_shape=jax.S...  39.2 us
    transpose x1, local copies, waits for them, and re-layouts, local(): return jnp.transpose(out, (1, 0, 2))  1.65 us

profile of v7, /device:TPU:0, one launch (start us, length us, event | category | flops | bytes accessed | tf_op | source)
XLA Modules:
  0.0 40.9 jit_solution(9987992217247007731)
XLA Ops:
  0.0 39.2 %shard_map.28 = bf16[8,512,128]{2,1,0:T(8,128)(2,1)S(1)} custom-call(bf16[128,1536]{1,0:T(8,128)(2,1)} %dens_hbm.1, s32[1,12]{1,0:T(1,128)} %pat_hbm.1), custom_call_target="tpu_custom_call" | custom-call | flops 1610612736 | bytes 1048576 | tf_op jit(solution)/shard_map/pallas_call | solution.py:478
  39.2 1.6 %copy.3 = bf16[512,8,128]{2,1,0:T(8,128)(2,1)} copy(bf16[512,8,128]{2,0,1:T(8,128)(2,1)S(1)} %bitcast.1) | data formatting | bytes 2097152 | tf_op jit(solution)/shard_map/transpose | solution.py:511

commit v8 on v6

--- a/solution.py
+++ b/solution.py
@@ -10,7 +10,6 @@
 MESH = pl.DeviceIdType.MESH
 CHUNKS = 4
 HALF = CHUNKS // 2
-LAST = CHUNKS * 3 // 4
 EARLY = CHUNKS // 4
 LAG = 2
 
@@ -64,6 +63,8 @@
         greet(dev_y(d))
     when(z > 0, lambda: greet(dev_z(z - 1)))
     when(z < zn - 1, lambda: greet(dev_z(z + 1)))
+    when(edge | (z == 2), lambda: greet(dev_z(jnp.where(edge, z + 2 * away, 0))))
+    when(inner & (z == zn - 3), lambda: greet(dev_z(zn - 1)))
 
     def rows_at(xx, n):
         return pl.ds(pl.multiple_of(xx * length + n * part, part), part)
@@ -104,8 +105,11 @@
     def down(zz, n):
         return row_copy(zz, x, n, s_dn.at[zz, n], dev_z(z - 1))
 
-    def double(zz, n):
-        return row_copy(zz, 1 - x, n, s_dup.at[jnp.where(zz == z, 0, 1), n], dev_z(inward))
+    def double(n):
+        return row_copy(z, 1 - x, n, s_dup.at[0, n], dev_z(inward))
+
+    def direct(n):
+        return row_copy(z, x, n, s_dup.at[1, n], dev_z(z + 2 * away))
 
     def across(zz, n):
         return row_copy(zz, x, n, s_x.at[zz, n], dev_x)
@@ -161,6 +165,10 @@
         if n == CHUNKS - 1:
             do(to_twin(0))
 
+    def late_sends(do):
+        for n in range(HALF, CHUNKS):
+            do(across(z, n))
+
     def y_arrivals(do, wait):
         for d in range(1, yn):
             if wait:
@@ -175,24 +183,19 @@
             do(edge_to_twin(d, n))
 
     def relay(zz, n, do):
-        @pl.when((zz < z) & (z + 1 <= zn - 2))
+        adjacent = proxy & (zz == ze)
+
+        @pl.when((zz < z) & (z + 1 <= zn - 2) & jnp.logical_not(adjacent))
         def _():
             do(up(zz, n))
 
-        @pl.when((zz > z) & (z - 1 >= 1))
+        @pl.when((zz > z) & (z - 1 >= 1) & jnp.logical_not(adjacent))
         def _():
             do(down(zz, n))
 
-        dist = jnp.abs(zz - z)
-        twice = ((zz == 0) | (zz == zn - 1)) & (
-            (dist == 1) | ((dist == 2) & (n >= LAST))
-        )
-
-        @pl.when(jnp.logical_not(twice))
+        @pl.when(jnp.logical_not(adjacent))
         def _():
             do(across(zz, n))
-
-        adjacent = proxy & (zz == ze)
 
         @pl.when(adjacent)
         def _():
@@ -257,7 +260,9 @@
         lax.fori_loop(low_d, high_d, body, 0)
 
     neighbours = 2 + (yn - 1)
-    pl.semaphore_wait(barrier, neighbours + jnp.where(edge, 1, 2))
+    pl.semaphore_wait(barrier, neighbours + jnp.where(
+        edge, 2, 2 + jnp.where(z == 2, 1, 0) + jnp.where(z == zn - 3, 1, 0)
+    ))
 
     for n in range(CHUNKS):
         own_sends(n, start)
@@ -270,8 +275,10 @@
     @pl.when(edge)
     def _():
         for n in range(CHUNKS):
+            direct(n).start()
+        for n in range(CHUNKS):
             got_row(z, 1 - x, n)
-            double(z, n).start()
+            double(n).start()
             got_row(inward, x, n)
             across(inward, n).start()
         y_arrivals(start, True)
@@ -283,8 +290,6 @@
             def _():
                 for n in range(CHUNKS):
                     got_row(inward, 1 - x, n)
-                    if n >= HALF:
-                        double(inward, n).start()
 
             own_job(jnp.where(j == 0, z, inward))
             return carry
@@ -293,10 +298,9 @@
 
         for n in range(CHUNKS):
             own_sends(n, finish)
-            double(z, n).wait_send()
+            double(n).wait_send()
+            direct(n).wait_send()
             across(inward, n).wait_send()
-            if n >= HALF:
-                double(inward, n).wait_send()
         own_sideways(range(CHUNKS), finish)
         y_arrivals(finish, False)
 
@@ -325,8 +329,7 @@
             def _():
                 for n in range(CHUNKS):
                     edge_arrivals(n, finish, False)
-                for n in range(LAST, CHUNKS):
-                    double(ze, n).wait_send()
+                late_sends(finish)
 
             def relayed(zz, carry):
                 @pl.when(zz != z)
@@ -351,12 +354,6 @@
                     def _():
                         got_row(zz, x, n)
                         relay(zz, n, start)
-
-                @pl.when(second & proxy)
-                def _():
-                    got_row(ze, 1 - x, n)
-                    if n >= LAST:
-                        double(ze, n).start()
 
             def proxied(dist, xx, low_d=0, high_d=yn):
                 @pl.when(proxy & (dist >= 1) & inside(z + dist * away))
@@ -396,6 +393,8 @@
                     got_edge_twin(d)
                 proxied(t, x, 1)
 
+            when(second & proxy, functools.partial(late_sends, start))
+
             @pl.when(t > 1)
             def _():
                 proxied(t, x)
@@ -409,14 +408,17 @@
 
             def own(j, inner_carry):
                 zz = z + jnp.where(j == 0, 1 - t, jnp.where(j == 1, t - 1, 0)) * away
-                last = j == 2
-
-                @pl.when(last & (t == zn - 1))
+                zz = jnp.where(j == 3, ze, zz)
+                late = j >= 2
+                now = jnp.where(late, t == zn - 1, jnp.logical_not(proxy & (zz == ze)))
+                now &= (j < 3) | proxy
+
+                @pl.when(late & now)
                 def _():
                     for n in range(CHUNKS):
-                        got_row(z, 1 - x, n)
-
-                @pl.when(inside(zz) & (jnp.logical_not(last) | (t == zn - 1)))
+                        got_row(zz, 1 - x, n)
+
+                @pl.when(inside(zz) & now)
                 def _():
                     own_job(zz)
 
@@ -424,7 +426,7 @@
 
             @pl.when(t > 1)
             def _():
-                lax.fori_loop(0, 3, own, 0)
+                lax.fori_loop(0, 4, own, 0)
 
             return carry
 

time: 37.6 us -> 43.5 us (1.16)
  Pallas kernels: 35.9 us -> 41.7 us
    pallas_call x1, Pallas kernels: 35.9 us -> 41.7 us  [local(): pl.pallas_call(functools.partial(kernel, rows_n, cols_n), out_shape=jax.S...]
where the time goes in v8:
time: 43.5 us; the launch traced here: 43.3 us
  Pallas kernels  41.7 us (96%)
  local copies, waits for them, and re-layouts  1.65 us (4%)
    pallas_call x1, Pallas kernels, local(): pl.pallas_call(functools.partial(kernel, rows_n, cols_n), out_shape=jax.S...  41.7 us
    transpose x1, local copies, waits for them, and re-layouts, local(): return jnp.transpose(out, (1, 0, 2))  1.65 us

profile of v8, /device:TPU:0, one launch (start us, length us, event | category | flops | bytes accessed | tf_op | source)
XLA Modules:
  0.0 43.3 jit_solution(3851727155810916901)
XLA Ops:
  0.0 41.7 %shard_map.28 = bf16[8,512,128]{2,1,0:T(8,128)(2,1)S(1)} custom-call(bf16[128,1536]{1,0:T(8,128)(2,1)} %dens_hbm.1, s32[1,12]{1,0:T(1,128)} %pat_hbm.1), custom_call_target="tpu_custom_call" | custom-call | flops 1610612736 | bytes 1048576 | tf_op jit(solution)/shard_map/pallas_call | solution.py:454
  41.7 1.6 %copy.3 = bf16[512,8,128]{2,1,0:T(8,128)(2,1)} copy(bf16[512,8,128]{2,0,1:T(8,128)(2,1)S(1)} %bitcast.1) | data formatting | bytes 2097152 | tf_op jit(solution)/shard_map/transpose | solution.py:487

commit v9 on v6

--- a/solution.py
+++ b/solution.py
@@ -11,7 +11,7 @@
 CHUNKS = 4
 HALF = CHUNKS // 2
 LAST = CHUNKS * 3 // 4
-EARLY = CHUNKS // 4
+EARLY = CHUNKS // 2
 LAG = 2
 
 def kernel(
@@ -401,30 +401,32 @@
                 proxied(t, x)
                 got_other(z - (t - 1) * away)
 
-            @pl.when(second)
-            def _():
-                y_arrivals(start, True)
+            when(second, functools.partial(y_arrivals, start, True))
+
+            @pl.when(t == 3)
+            def _():
                 for d in range(yn):
                     got_twin(d)
 
             def own(j, inner_carry):
-                zz = z + jnp.where(j == 0, 1 - t, jnp.where(j == 1, t - 1, 0)) * away
-                last = j == 2
-
-                @pl.when(last & (t == zn - 1))
+                dist = jnp.where(j < 2, t - 2, jnp.where(j < 4, t - 1, 0))
+                zz = z + jnp.where(lax.rem(j, 2) == 0, dist, -dist) * away
+                last = t == zn - 1
+
+                @pl.when((j == 4) & last)
                 def _():
                     for n in range(CHUNKS):
                         got_row(z, 1 - x, n)
 
-                @pl.when(inside(zz) & (jnp.logical_not(last) | (t == zn - 1)))
+                @pl.when(inside(zz) & ((j < 2) | last))
                 def _():
                     own_job(zz)
 
                 return inner_carry
 
-            @pl.when(t > 1)
-            def _():
-                lax.fori_loop(0, 3, own, 0)
+            @pl.when(t > 2)
+            def _():
+                lax.fori_loop(0, 5, own, 0)
 
             return carry
 

time: 37.6 us -> 37.7 us (level)
  no operation moved by 1% of the time
where the time goes in v9:
time: 37.7 us; the launch traced here: 37.6 us
  Pallas kernels  35.9 us (95%)
  local copies, waits for them, and re-layouts  1.65 us (4%)
    pallas_call x1, Pallas kernels, local(): pl.pallas_call(functools.partial(kernel, rows_n, cols_n), out_shape=jax.S...  35.9 us
    transpose x1, local copies, waits for them, and re-layouts, local(): return jnp.transpose(out, (1, 0, 2))  1.65 us

profile of v9, /device:TPU:0, one launch (start us, length us, event | category | flops | bytes accessed | tf_op | source)
XLA Modules:
  0.0 37.6 jit_solution(4476826513378602581)
XLA Ops:
  0.0 35.9 %shard_map.28 = bf16[8,512,128]{2,1,0:T(8,128)(2,1)S(1)} custom-call(bf16[128,1536]{1,0:T(8,128)(2,1)} %dens_hbm.1, s32[1,12]{1,0:T(1,128)} %pat_hbm.1), custom_call_target="tpu_custom_call" | custom-call | flops 1610612736 | bytes 1048576 | tf_op jit(solution)/shard_map/pallas_call | solution.py:454
  35.9 1.6 %copy.3 = bf16[512,8,128]{2,1,0:T(8,128)(2,1)} copy(bf16[512,8,128]{2,0,1:T(8,128)(2,1)S(1)} %bitcast.1) | data formatting | bytes 2097152 | tf_op jit(solution)/shard_map/transpose | solution.py:487

commit v10 on v4

--- a/solution.py
+++ b/solution.py
@@ -8,7 +8,7 @@
 from jax.sharding import PartitionSpec as P
 
 MESH = pl.DeviceIdType.MESH
-CHUNKS = 4
+CHUNKS = 2
 HALF = CHUNKS // 2
 LAST = CHUNKS - 1
 

time: 37.2 us -> 38.2 us (1.027)
  Pallas kernels: 35.4 us -> 36.4 us
    pallas_call x1, Pallas kernels: 35.4 us -> 36.4 us  [local(): pl.pallas_call(functools.partial(kernel, rows_n, cols_n), out_shape=jax.S...]
where the time goes in v10:
time: 38.2 us; the launch traced here: 38 us
  Pallas kernels  36.4 us (95%)
  local copies, waits for them, and re-layouts  1.65 us (4%)
    pallas_call x1, Pallas kernels, local(): pl.pallas_call(functools.partial(kernel, rows_n, cols_n), out_shape=jax.S...  36.4 us
    transpose x1, local copies, waits for them, and re-layouts, local(): return jnp.transpose(out, (1, 0, 2))  1.65 us

profile of v10, /device:TPU:0, one launch (start us, length us, event | category | flops | bytes accessed | tf_op | source)
XLA Modules:
  0.0 38.0 jit_solution(2193338124886217722)
XLA Ops:
  0.0 36.4 %shard_map.28 = bf16[8,512,128]{2,1,0:T(8,128)(2,1)S(1)} custom-call(bf16[128,1536]{1,0:T(8,128)(2,1)} %dens_hbm.1, s32[1,12]{1,0:T(1,128)} %pat_hbm.1), custom_call_target="tpu_custom_call" | custom-call | flops 1610612736 | bytes 1048576 | tf_op jit(solution)/shard_map/pallas_call | solution.py:445
  36.4 1.6 %copy.3 = bf16[512,8,128]{2,1,0:T(8,128)(2,1)} copy(bf16[512,8,128]{2,0,1:T(8,128)(2,1)S(1)} %bitcast.1) | data formatting | bytes 2097152 | tf_op jit(solution)/shard_map/transpose | solution.py:478

commit v11 on v4

--- a/solution.py
+++ b/solution.py
@@ -10,7 +10,7 @@
 MESH = pl.DeviceIdType.MESH
 CHUNKS = 4
 HALF = CHUNKS // 2
-LAST = CHUNKS - 1
+LAST = CHUNKS
 
 
 def kernel(
@@ -372,7 +372,7 @@
                 proxied(t - 1, x, 1)
 
             for n in range(HALF, CHUNKS):
-                if n == LAST:
+                if n == CHUNKS - 1:
                     @pl.when(t > 1)
                     def _():
                         got_other(z + (t - 1) * away)

time: 37.2 us -> 37.2 us (level)
  no operation moved by 1% of the time
where the time goes in v11:
time: 37.2 us; the launch traced here: 37.1 us
  Pallas kernels  35.4 us (95%)
  local copies, waits for them, and re-layouts  1.65 us (4%)
    pallas_call x1, Pallas kernels, local(): pl.pallas_call(functools.partial(kernel, rows_n, cols_n), out_shape=jax.S...  35.4 us
    transpose x1, local copies, waits for them, and re-layouts, local(): return jnp.transpose(out, (1, 0, 2))  1.65 us

profile of v11, /device:TPU:0, one launch (start us, length us, event | category | flops | bytes accessed | tf_op | source)
XLA Modules:
  0.0 37.1 jit_solution(1096340686429992431)
XLA Ops:
  0.0 35.4 %shard_map.28 = bf16[8,512,128]{2,1,0:T(8,128)(2,1)S(1)} custom-call(bf16[128,1536]{1,0:T(8,128)(2,1)} %dens_hbm.1, s32[1,12]{1,0:T(1,128)} %pat_hbm.1), custom_call_target="tpu_custom_call" | custom-call | flops 1610612736 | bytes 1048576 | tf_op jit(solution)/shard_map/pallas_call | solution.py:445
  35.5 1.6 %copy.3 = bf16[512,8,128]{2,1,0:T(8,128)(2,1)} copy(bf16[512,8,128]{2,0,1:T(8,128)(2,1)S(1)} %bitcast.1) | data formatting | bytes 2097152 | tf_op jit(solution)/shard_map/transpose | solution.py:478
